TPU v7x, 512 devices: a whole 4x4x16 slice. The times are simulated.
512 devices in a mesh: seq: 64 (over z_lo, x, core), dp: 8 (over z_hi, y).
Axes of the slice: x: 4, y: 4, z: 16 (z_hi: 2, z_lo: 8; z = z_hi * 8 + z_lo), core: 2. Of those that a mesh axis runs over, the one named last changes fastest.
Arguments:
- layer_in: bfloat16 [4096, 16384], P('dp', 'seq'), may hold values from -6 to 6
- cotangent: bfloat16 [4096, 16384], P('dp', 'seq'), may hold values from -16 to 16
- value_taps: float32 [3, 4096], P(None, 'dp'), may hold values from -3.5 to 3.5
- gate_taps: float32 [3, 4096], P(None, 'dp'), may hold values from -3.5 to 3.5
- long_filter: bfloat16 [256, 16384], P('dp', 'seq'), may hold values from -2 to 2
Outputs:
- layer_out: bfloat16 [4096, 16384], P('dp', 'seq')
- input_grad: bfloat16 [4096, 16384], P('dp', 'seq')
- value_tap_grad: float32 [3, 4096], P(None, 'dp')
- gate_tap_grad: float32 [3, 4096], P(None, 'dp')
- filter_grad: float32 [256, 16384], P('dp', 'seq')
All inputs are finite; a program needn't handle non-finite values.
Results may differ from a plain program's by a relative error of at most 0.0062.
Values may be sent and summed in bfloat16 or wider, within the bound.
A program may use at most 64 MiB of HBM per device.

v0:
```python
from functools import partial
import math

import jax
import jax.numpy as jnp
from jax import lax
from jax.sharding import PartitionSpec as P

GROUP = 16


def passed_along(value, axis, steps):
    count = lax.axis_size(axis)
    leading, last = (max(0, -steps), min(count, count - steps))
    return lax.ppermute(value, axis, [(source, source + steps) for source in range(leading, last)])


def causal_mix(extended, taps, cols):
    return (
        taps[0][:, None] * extended[:, 2 : 2 + cols]
        + taps[1][:, None] * extended[:, 1 : 1 + cols]
        + taps[2][:, None] * extended[:, 0:cols]
    )


def adjoint_mix(extended, taps, cols):
    return (
        taps[0][:, None] * extended[:, 0:cols]
        + taps[1][:, None] * extended[:, 1 : 1 + cols]
        + taps[2][:, None] * extended[:, 2 : 2 + cols]
    )


def tap_terms(grad, extended, cols):
    return jnp.stack(
        [
            jnp.sum(grad * extended[:, 2 - shift_by : 2 - shift_by + cols], axis=1)
            for shift_by in range(3)
        ]
    )


def dft_tables(blocks, cols):
    n_fft = 2 * blocks * cols
    freq_rows = jnp.arange(2 * blocks, dtype=jnp.int32)
    block_ids = jnp.arange(blocks, dtype=jnp.int32)
    col_ids = jnp.arange(cols, dtype=jnp.int32)
    outer = (
        2.0
        * math.pi
        / (2 * blocks)
        * (freq_rows[:, None] * block_ids[None, :] % (2 * blocks)).astype(jnp.float32)
    )
    twist = (
        2.0 * math.pi / n_fft * (freq_rows[:, None] * col_ids[None, :] % n_fft).astype(jnp.float32)
    )
    inner = 2.0 * math.pi / cols * (col_ids[:, None] * col_ids[None, :] % cols).astype(jnp.float32)
    return (
        jnp.cos(outer),
        jnp.sin(outer),
        jnp.cos(twist),
        jnp.sin(twist),
        jnp.cos(inner),
        jnp.sin(inner),
    )


def forward_spectrum(real_part, imag_part, tables):
    cos_outer, sin_outer, cos_twist, sin_twist, cos_inner, sin_inner = tables
    product = partial(jnp.einsum, precision=lax.Precision.HIGHEST)
    first_re = product("ka,cab->ckb", cos_outer, real_part) + product(
        "ka,cab->ckb", sin_outer, imag_part
    )
    first_im = product("ka,cab->ckb", cos_outer, imag_part) - product(
        "ka,cab->ckb", sin_outer, real_part
    )
    turned_re = cos_twist * first_re + sin_twist * first_im
    turned_im = cos_twist * first_im - sin_twist * first_re
    spec_re = product("ckb,bm->ckm", turned_re, cos_inner) + product(
        "ckb,bm->ckm", turned_im, sin_inner
    )
    spec_im = product("ckb,bm->ckm", turned_im, cos_inner) - product(
        "ckb,bm->ckm", turned_re, sin_inner
    )
    return (spec_re, spec_im)


def inverse_spectrum(spec_re, spec_im, tables, real_only):
    cos_outer, sin_outer, cos_twist, sin_twist, cos_inner, sin_inner = tables
    product = partial(jnp.einsum, precision=lax.Precision.HIGHEST)
    n_fft = spec_re.shape[1] * spec_re.shape[2]
    back_re = product("ckm,bm->ckb", spec_re, cos_inner) - product(
        "ckm,bm->ckb", spec_im, sin_inner
    )
    back_im = product("ckm,bm->ckb", spec_im, cos_inner) + product(
        "ckm,bm->ckb", spec_re, sin_inner
    )
    turned_re = cos_twist * back_re - sin_twist * back_im
    turned_im = cos_twist * back_im + sin_twist * back_re
    out_re = (
        product("ka,ckb->cab", cos_outer, turned_re) - product("ka,ckb->cab", sin_outer, turned_im)
    ) / n_fft
    if real_only:
        return out_re
    out_im = (
        product("ka,ckb->cab", cos_outer, turned_im) + product("ka,ckb->cab", sin_outer, turned_re)
    ) / n_fft
    return (out_re, out_im)


def mirror(spec):
    flipped = jnp.roll(jnp.flip(spec, 1), 1, axis=1)
    plain = jnp.flip(flipped, 2)
    first_row = jnp.roll(plain, 1, axis=2)
    row_ids = jnp.arange(spec.shape[1], dtype=jnp.int32)[None, :, None]
    return jnp.where(row_ids == 0, first_row, plain)


def channel_work(values, grad_z, filt, blocks, scale):
    chans, seq_len = values.shape
    cols = seq_len // blocks
    groups = filt.shape[0]
    group_size = chans // groups
    tables = dft_tables(blocks, cols)
    pack_re, pack_im = forward_spectrum(
        values.astype(jnp.float32).reshape(chans, blocks, cols),
        grad_z.astype(jnp.float32).reshape(chans, blocks, cols),
        tables,
    )
    back_re = mirror(pack_re)
    back_im = mirror(pack_im)
    shape4 = (groups, group_size, 2 * blocks, cols)
    value_re = (0.5 * (pack_re + back_re)).reshape(shape4)
    value_im = (0.5 * (pack_im - back_im)).reshape(shape4)
    grad_re = (0.5 * (pack_im + back_im)).reshape(shape4)
    grad_im = (0.5 * (back_re - pack_re)).reshape(shape4)
    filt_f = filt.astype(jnp.float32).reshape(groups, blocks, cols)
    filt_re, filt_im = forward_spectrum(filt_f, jnp.zeros_like(filt_f), tables)
    filt_re = filt_re[:, None]
    filt_im = filt_im[:, None]
    conv_re = filt_re * value_re - filt_im * value_im
    conv_im = filt_re * value_im + filt_im * value_re
    corr_re = filt_re * grad_re + filt_im * grad_im
    corr_im = filt_re * grad_im - filt_im * grad_re
    joined_re = (conv_re - corr_im).reshape(chans, 2 * blocks, cols)
    joined_im = (conv_im + corr_re).reshape(chans, 2 * blocks, cols)
    cross_re = jnp.sum(value_re * grad_re + value_im * grad_im, axis=1)
    cross_im = jnp.sum(value_re * grad_im - value_im * grad_re, axis=1)
    conv_out, grad_out = inverse_spectrum(joined_re, joined_im, tables, False)
    filt_out = inverse_spectrum(cross_re, cross_im, tables, True)
    conv_chan = conv_out.reshape(chans, seq_len).astype(jnp.bfloat16)
    grad_chan = grad_out.reshape(chans, seq_len).astype(jnp.bfloat16)
    return (conv_chan, grad_chan, filt_out.reshape(groups, seq_len) * scale)


def per_device(layer_in, cotangent, value_taps, gate_taps, long_filter):
    chans, cols = layer_in.shape
    blocks = lax.axis_size("seq")
    replicas = lax.axis_size("dp")
    seq_len = blocks * cols
    filters_here = long_filter.shape[0]
    group_size = chans // filters_here
    chans_after = chans // blocks
    copies = max(1, group_size // chans_after)
    filt_rep = jnp.repeat(long_filter, copies, axis=0)
    filt_scale = 1.0 / math.sqrt(GROUP * seq_len)
    upstream = cotangent.astype(jnp.float32)
    before = passed_along(layer_in[:, cols - 2 :], "seq", 1)
    extended = jnp.concatenate([before, layer_in], axis=1).astype(jnp.float32)
    values = causal_mix(extended, value_taps, cols).astype(jnp.bfloat16)
    gate = causal_mix(extended, gate_taps, cols)
    grad_z = (gate * upstream).astype(jnp.bfloat16)
    values_chan, grad_chan, filt_chan = (
        lax.all_to_all(values, "seq", split_axis=0, concat_axis=1, tiled=True),
        lax.all_to_all(grad_z, "seq", split_axis=0, concat_axis=1, tiled=True),
        lax.all_to_all(filt_rep, "seq", split_axis=0, concat_axis=1, tiled=True),
    )
    conv_chan, grad_s_chan, filt_part = channel_work(
        values_chan, grad_chan, filt_chan, blocks, filt_scale
    )
    conv_seq, grad_s = (
        lax.all_to_all(conv_chan, "seq", split_axis=1, concat_axis=0, tiled=True),
        lax.all_to_all(grad_s_chan, "seq", split_axis=1, concat_axis=0, tiled=True),
    )
    conv_wide = conv_seq.astype(jnp.float32)
    layer_out = (gate * conv_wide).astype(jnp.bfloat16)
    grad_g = (conv_wide * upstream).astype(jnp.bfloat16)
    after_s, after_g = passed_along((grad_s[:, :2], grad_g[:, :2]), "seq", -1)
    grad_s_ext = jnp.concatenate([grad_s, after_s], axis=1).astype(jnp.float32)
    grad_g_ext = jnp.concatenate([grad_g, after_g], axis=1).astype(jnp.float32)
    input_grad = (
        adjoint_mix(grad_s_ext, value_taps, cols) + adjoint_mix(grad_g_ext, gate_taps, cols)
    ).astype(jnp.bfloat16)
    partials = jnp.stack(
        [
            tap_terms(grad_s_ext[:, :cols], extended, cols),
            tap_terms(grad_g_ext[:, :cols], extended, cols),
        ]
    )
    tap_raw = lax.psum(partials, "seq")
    filt_seq = lax.all_to_all(filt_part, "seq", split_axis=1, concat_axis=0, tiled=True)
    filter_grad = jnp.sum(filt_seq.reshape(filters_here, copies, cols), axis=1)
    squares = jnp.sum(tap_raw * tap_raw)
    total = lax.psum(squares, "dp")
    tap_scale = lax.rsqrt(total / jnp.float32(6 * chans * replicas) + 1e-05)
    return (layer_out, input_grad, tap_raw[0] * tap_scale, tap_raw[1] * tap_scale, filter_grad)


def solution(mesh):
    placed = (P("dp", "seq"), P("dp", "seq"), P(None, "dp"), P(None, "dp"), P("dp", "seq"))
    return jax.shard_map(
        per_device,
        mesh=mesh,
        in_specs=placed,
        out_specs=(P("dp", "seq"), P("dp", "seq"), P(None, "dp"), P(None, "dp"), P("dp", "seq")),
        check_vma=False,
    )
```

profile of v0, /device:TPU:0, one launch (start us, length us, event | category | flops | bytes accessed | tf_op | source)
XLA Modules:
  0.0 714.7 jit_solution(15510648283955671899)
XLA Ops:
  1.7 1.4 collective-permute-start
  5.2 12.3 %all-to-all-start.2 = ((bf16[64,2,128]{2,1,0:T(2,128)(2,1)}), bf16[64,2,128]{2,1,0:T(2,128)(2,1)S(1)}, u32[]{:S(2)}, u32[]{:S(2)}) async-start(bf16[64,2,128]{2,1,0:T(2,128)(2,1)} %reshape.244), calls=%async_computation.2 | async-start | bytes 65536 | tf_op jit(solution)/shard_map/all_to_all | solution.py:176
  19.1 1.7 fusion.33
  20.8 9.0 %all-to-all-done.2 = bf16[64,2,128]{2,1,0:T(2,128)(2,1)S(1)} async-done(((bf16[64,2,128]{2,1,0:T(2,128)(2,1)}), bf16[64,2,128]{2,1,0:T(2,128)(2,1)S(1)}, u32[]{:S(2)}, u32[]{:S(2)}) %all-to-all-start.2) | async-done | bytes 32800 | tf_op jit(solution)/shard_map/all_to_all | solution.py:176
  29.8 4.6 all-to-all-start.1
  36.8 17.4 %all-to-all-done.1 = bf16[64,8,256]{2,1,0:T(8,128)(2,1)S(1)} async-done(((bf16[64,8,256]{2,1,0:T(8,128)(2,1)}), bf16[64,8,256]{2,1,0:T(8,128)(2,1)S(1)}, u32[]{:S(2)}, u32[]{:S(2)}) %all-to-all-start.1) | async-done | bytes 262176 | tf_op jit(solution)/shard_map/all_to_all | solution.py:175
  54.3 6.1 all-to-all-start
  60.4 1.8 fusion.67
  62.2 1.8 fusion.71
  64.0 2.4 fusion.8
  66.4 2.4 fusion.9
  69.6 10.4 %all-to-all-done = bf16[64,8,256]{2,1,0:T(8,128)(2,1)S(1)} async-done(((bf16[64,8,256]{2,1,0:T(8,128)(2,1)}), bf16[64,8,256]{2,1,0:T(8,128)(2,1)S(1)}, u32[]{:S(2)}, u32[]{:S(2)}) %all-to-all-start) | async-done | bytes 262176 | tf_op jit(solution)/shard_map/all_to_all | solution.py:174
  81.5 1.7 fusion
  83.9 2.9 fusion.44
  86.9 2.7 convolution_add_fusion.1
  91.0 8.9 %slice.133 = f32[8,127,256]{2,1,0:T(8,128)} reverse(f32[8,127,256]{2,1,0:T(8,128)} %slice.157), dimensions={1} | reverse | bytes 2080768 | tf_op jit(solution)/shard_map/jit(_roll_static)/slice | solution.py:112
  99.9 2.7 fusion.17
  103.7 2.7 fusion.42
  106.4 2.7 convolution_subtract_fusion.1
  110.5 7.1 slice.139
  118.8 1.4 fusion.16
  121.7 5.8 reverse.8
  127.6 2.6 slice.252
  130.2 5.8 rev.10
  136.1 1.4 reverse.9
  138.8 9.9 %rev.11 = f32[8,128,256]{2,1,0:T(8,128)} reverse(f32[8,128,256]{2,1,0:T(8,128)} %pad_maximum_fusion.1), dimensions={2} | reverse | bytes 2097152 | tf_op jit(solution)/shard_map/jit(_flip)/rev | solution.py:113
  148.7 5.4 add_reduce_fusion
  154.1 1.3 fusion.87
  156.8 1.4 convolution_subtract_fusion.4
  158.2 1.4 convolution_add_fusion.4
  162.0 6.2 all-to-all-start.5
  168.2 2.0 subtract_subtract_fusion
  170.3 2.1 fusion.40
  172.3 2.1 fusion.38
  174.4 2.1 convolution_subtract_fusion
  176.5 2.1 convolution_add_fusion
  178.6 1.5 fusion.59
  180.1 1.5 fusion.7
  182.4 13.3 %all-to-all-start.3 = ((bf16[8,64,256]{2,0,1:T(8,128)(2,1)}), bf16[8,64,256]{2,0,1:T(8,128)(2,1)S(1)}, u32[]{:S(2)}, u32[]{:S(2)}) async-start(bf16[8,64,256]{2,0,1:T(8,128)(2,1)} %copy.76), calls=%async_computation.3 | async-start | bytes 524288 | tf_op jit(solution)/shard_map/all_to_all | solution.py:182
  195.7 1.5 fusion.60
  197.2 1.5 fusion.6
  199.6 15.9 %all-to-all-done.3 = bf16[8,64,256]{2,0,1:T(8,128)(2,1)S(1)} async-done(((bf16[8,64,256]{2,0,1:T(8,128)(2,1)}), bf16[8,64,256]{2,0,1:T(8,128)(2,1)S(1)}, u32[]{:S(2)}, u32[]{:S(2)}) %all-to-all-start.3) | async-done | bytes 262176 | tf_op jit(solution)/shard_map/all_to_all | solution.py:182
  215.5 6.0 all-to-all-start.4
  223.9 17.4 %all-to-all-done.4 = bf16[8,64,256]{2,0,1:T(8,128)(2,1)S(1)} async-done(((bf16[8,64,256]{2,0,1:T(8,128)(2,1)}), bf16[8,64,256]{2,0,1:T(8,128)(2,1)S(1)}, u32[]{:S(2)}, u32[]{:S(2)}) %all-to-all-start.4) | async-done | bytes 262176 | tf_op jit(solution)/shard_map/all_to_all | solution.py:183
  242.7 1.9 collective-permute-done.1
  244.6 2.5 multiply_reduce_fusion.5
  247.2 421.9 %psum.14 = f32[2,3,512]{2,1,0:T(4,128)S(1)} all-reduce(f32[2,3,512]{2,1,0:T(4,128)S(1)} %pad_maximum_fusion.2), channel_id=1, replica_groups=mesh['seq'=64,'dp'=8] {'seq'}, use_global_device_ids=true, to_apply=%region_8.9 | all-reduce | flops 3072 | bytes 24576 | tf_op jit(solution)/shard_map/psum | solution.py:200
  670.4 42.7 %psum.15 = f32[]{:T(128)} all-reduce(f32[]{:T(128)} %multiply_reduce_fusion.8), channel_id=1, replica_groups=mesh['seq'=64,'dp'=8] {'dp'}, use_global_device_ids=true, to_apply=%region_10.11 | all-reduce | flops 1 | bytes 8 | tf_op jit(solution)/shard_map/psum | solution.py:204
  (96 shorter events, 28.9 us)
Async XLA Ops:
  0.6 2.5 copy-start.18
  1.7 16.5 %copy-start.15 = (bf16[512,256]{1,0:T(8,128)(2,1)S(1)}, bf16[512,256]{1,0:T(8,128)(2,1)}, u32[]{:S(2)}) copy-start(bf16[512,256]{1,0:T(8,128)(2,1)} %param.5) | copy-start | bytes 786436
  1.7 16.5 %collective-permute-start = (bf16[512,2]{1,0:T(8,128)(2,1)S(1)}, bf16[512,2]{1,0:T(8,128)(2,1)S(1)}, u32[]{:S(2)}, u32[]{:S(2)}) collective-permute-start(bf16[512,2]{1,0:T(8,128)(2,1)S(1)} %slice.122), channel_id=1, source_target_pairs={{0,8},{8,16},{16,24},{24,32},{32,40},{40,48},{48,56},{56,64},{64,7... | collective-permute-start | bytes 6152 | tf_op jit(solution)/shard_map/ppermute | solution.py:15
  5.1 12.3 %copy-start.19 = (f32[3,512]{1,0:T(4,128)S(1)}, f32[3,512]{1,0:T(4,128)}, u32[]{:S(2)}) copy-start(f32[3,512]{1,0:T(4,128)} %param.8) | copy-start | bytes 18436
  5.2 24.7 %all-to-all-start.2 = ((bf16[64,2,128]{2,1,0:T(2,128)(2,1)}), bf16[64,2,128]{2,1,0:T(2,128)(2,1)S(1)}, u32[]{:S(2)}, u32[]{:S(2)}) async-start(bf16[64,2,128]{2,1,0:T(2,128)(2,1)} %reshape.244), calls=%async_computation.2 | async-start | bytes 65536 | tf_op jit(solution)/shard_map/all_to_all | solution.py:176
  17.5 0.7 copy-start.20
  18.2 0.9 copy-start.13
  29.8 24.4 %all-to-all-start.1 = ((bf16[64,8,256]{2,1,0:T(8,128)(2,1)}), bf16[64,8,256]{2,1,0:T(8,128)(2,1)S(1)}, u32[]{:S(2)}, u32[]{:S(2)}) async-start(bf16[64,8,256]{2,1,0:T(8,128)(2,1)} %get-tuple-element.20), calls=%async_computation.1 | async-start | bytes 524288 | tf_op jit(solution)/shard_map/all_to_all | solution.py:175
  54.3 25.8 %all-to-all-start = ((bf16[64,8,256]{2,1,0:T(8,128)(2,1)}), bf16[64,8,256]{2,1,0:T(8,128)(2,1)S(1)}, u32[]{:S(2)}, u32[]{:S(2)}) async-start(bf16[64,8,256]{2,1,0:T(8,128)(2,1)} %get-tuple-element.25), calls=%async_computation | async-start | bytes 524288 | tf_op jit(solution)/shard_map/all_to_all | solution.py:174
  80.0 0.7 copy-start.11
  89.6 1.3 copy-start.2
  99.9 2.7 copy-start
  109.2 1.3 copy-start.4
  110.5 7.1 copy-start.1
  120.1 1.6 copy-start.9
  127.6 2.6 copy-start.8
  130.2 5.9 copy-start.10
  138.8 9.9 %copy-start.3 = (f32[8,128,256]{2,1,0:T(8,128)S(1)}, f32[8,128,256]{2,1,0:T(8,128)}, u32[]{:S(2)}) copy-start(f32[8,128,256]{2,1,0:T(8,128)} %copy-done.2) | copy-start | bytes 3145732
  138.8 9.9 %copy-start.5 = (f32[8,128,256]{2,1,0:T(8,128)S(1)}, f32[8,128,256]{2,1,0:T(8,128)}, u32[]{:S(2)}) copy-start(f32[8,128,256]{2,1,0:T(8,128)} %copy-done.4) | copy-start | bytes 3145732
  158.2 10.0 %copy-start.7 = (f32[8,128,256]{2,1,0:T(8,128)S(1)}, f32[8,128,256]{2,1,0:T(8,128)}, u32[]{:S(2)}) copy-start(f32[8,128,256]{2,1,0:T(8,128)} %get-tuple-element.17) | copy-start | bytes 3145732
  159.5 8.7 %copy-start.6 = (f32[8,128,256]{2,1,0:T(8,128)S(1)}, f32[8,128,256]{2,1,0:T(8,128)}, u32[]{:S(2)}) copy-start(f32[8,128,256]{2,1,0:T(8,128)} %get-tuple-element.16) | copy-start | bytes 3145732
  161.3 6.9 copy-start.16
  161.3 6.9 copy-start.17
  162.0 20.4 %all-to-all-start.5 = ((f32[1,64,256]{2,0,1:T(1,128)}), f32[1,64,256]{2,0,1:T(1,128)S(1)}, u32[]{:S(2)}, u32[]{:S(2)}) async-start(f32[1,64,256]{2,0,1:T(1,128)} %copy.80), calls=%async_computation.5 | async-start | bytes 131072 | tf_op jit(solution)/shard_map/all_to_all | solution.py:201
  182.4 33.1 %all-to-all-start.3 = ((bf16[8,64,256]{2,0,1:T(8,128)(2,1)}), bf16[8,64,256]{2,0,1:T(8,128)(2,1)S(1)}, u32[]{:S(2)}, u32[]{:S(2)}) async-start(bf16[8,64,256]{2,0,1:T(8,128)(2,1)} %copy.76), calls=%async_computation.3 | async-start | bytes 524288 | tf_op jit(solution)/shard_map/all_to_all | solution.py:182
  198.7 22.8 %copy-start.12 = (f32[512,256]{1,0:T(8,128)S(1)}, f32[512,256]{1,0:T(8,128)}, u32[]{:S(2)}) copy-start(f32[512,256]{1,0:T(8,128)} %get-tuple-element.21) | copy-start | bytes 1572868
  199.6 22.0 %copy-start.14 = (bf16[512,256]{1,0:T(8,128)(2,1)S(1)}, bf16[512,256]{1,0:T(8,128)(2,1)}, u32[]{:S(2)}) copy-start(bf16[512,256]{1,0:T(8,128)(2,1)} %param.6) | copy-start | bytes 786436
  215.5 25.8 %all-to-all-start.4 = ((bf16[8,64,256]{2,0,1:T(8,128)(2,1)}), bf16[8,64,256]{2,0,1:T(8,128)(2,1)S(1)}, u32[]{:S(2)}, u32[]{:S(2)}) async-start(bf16[8,64,256]{2,0,1:T(8,128)(2,1)} %copy.79), calls=%async_computation.4 | async-start | bytes 524288 | tf_op jit(solution)/shard_map/all_to_all | solution.py:183
  222.4 20.3 %collective-permute-start.2 = (bf16[512,2]{1,0:T(8,128)(2,1)S(1)}, bf16[512,2]{1,0:T(8,128)(2,1)S(1)}, u32[]{:S(2)}, u32[]{:S(2)}) collective-permute-start(bf16[512,2]{1,0:T(8,128)(2,1)S(1)} %slice.172), channel_id=1, source_target_pairs={{8,0},{16,8},{24,16},{32,24},{40,32},{48,40},{56,48},{64,56},{72,6... | collective-permute-start | bytes 6152 | tf_op jit(solution)/shard_map/ppermute | solution.py:15
  241.3 3.2 collective-permute-start.1
where the time goes:
time: 722 us; the launch traced here: 715 us
  blocking collectives  465 us (64%)
  waiting for transfers between devices  72.2 us (10%)
  local copies, waits for them, and re-layouts  53.2 us (7%)
  starting transfers between devices  52.5 us (7%)
  matrix products  45.7 us (6%)
  other arithmetic  24.3 us (3%)
    psum x1, blocking collectives, per_device(): tap_raw = lax.psum(partials, 'seq')  422 us
    psum x1, blocking collectives, per_device(): total = lax.psum(squares, 'dp')  42.7 us
    slice x6, local copies, waits for them, and re-layouts, mirror(): flipped = jnp.roll(jnp.flip(spec, 1), 1, axis=1)  18.5 us
    all_to_all x1, waiting for transfers between devices, per_device(): lax.all_to_all(grad_z, 'seq', split_axis=0, concat_axis=1, tiled=True)  17.4 us
    all_to_all x1, waiting for transfers between devices, per_device(): lax.all_to_all(grad_s_chan, 'seq', split_axis=1, concat_axis=0, tiled=True)  17.4 us
    all_to_all x1, waiting for transfers between devices, per_device(): lax.all_to_all(conv_chan, 'seq', split_axis=1, concat_axis=0, tiled=True)  15.9 us
    rev x2, local copies, waits for them, and re-layouts, mirror(): plain = jnp.flip(flipped, 2)  15.7 us
    unnamed x48, local copies, waits for them, and re-layouts  14.7 us
  transfers between devices with their start and end apart: 9, of which 6 were waited for; matrix products, arithmetic and copies ran while one was open for 5% of the time, Pallas kernels for 0%

commit v1 on v0

v1 whole, which is shorter than its diff:
```python
from functools import partial
import math

import jax
import jax.numpy as jnp
from jax import lax
from jax.experimental import pallas as pl
from jax.experimental.pallas import tpu as pltpu
from jax.sharding import PartitionSpec as P

GROUP = 16
LANES = 128
STACK = 4
MESH = pl.DeviceIdType.MESH
VMEM_LIMIT = 48 * 1024 * 1024
F32 = jnp.float32
BF16 = jnp.bfloat16


def greet(count):
    me = lax.axis_index("seq")
    barrier = pltpu.get_barrier_semaphore()

    @pl.loop(1, count)
    def _(step):
        peer = lax.rem(me + step, count)
        pl.semaphore_signal(barrier, inc=1, device_id={"seq": peer}, device_id_type=MESH)

    return barrier


def exchange_in(blocks, x_ref, u_ref, h_ref, xu_out, h_out, pack, got, hpack, hgot, sends, recvs):
    me = lax.axis_index("seq")
    barrier = greet(blocks)

    @pl.loop(0, blocks // 2)
    def _(pair):
        rows = pl.ds(pl.multiple_of(pair * 16, 16), 16)
        x = x_ref[rows, :].astype(F32)
        u = u_ref[rows, :].astype(F32)
        pack[2 * pair] = jnp.concatenate([x[:8], u[:8]], axis=0).astype(BF16)
        pack[2 * pair + 1] = jnp.concatenate([x[8:], u[8:]], axis=0).astype(BF16)

    taps = h_ref[...].astype(F32)
    for row in range(blocks // 2):
        hpack[row] = taps[row : row + 1]

    got[me] = pack[me]
    hgot[me] = hpack[me // 2]
    pl.semaphore_wait(barrier, blocks - 1)

    def copies(peer, source):
        return (
            pltpu.make_async_remote_copy(
                src_ref=hpack.at[peer // 2],
                dst_ref=hgot.at[source],
                send_sem=sends.at[0, peer],
                recv_sem=recvs.at[0, source],
                device_id={"seq": peer},
                device_id_type=MESH,
            ),
            pltpu.make_async_remote_copy(
                src_ref=pack.at[peer],
                dst_ref=got.at[source],
                send_sem=sends.at[1, peer],
                recv_sem=recvs.at[1, source],
                device_id={"seq": peer},
                device_id_type=MESH,
            ),
        )

    @pl.loop(1, blocks)
    def _(step):
        peer = lax.rem(me + step, blocks)
        for copy in copies(peer, me):
            copy.start()

    @pl.loop(1, blocks)
    def _(step):
        peer = lax.rem(me + step, blocks)
        for copy in copies(peer, peer):
            copy.wait_send()
            copy.wait_recv()

    xu_out[...] = got[...]
    h_out[...] = hgot[...]


def column(taps_ref, row, start):
    width = taps_ref.shape[1]
    wide = jnp.broadcast_to(taps_ref[row : row + 1, :], (8, width))
    lane = lax.broadcasted_iota(jnp.int32, (8, width), 1)
    chan = lax.broadcasted_iota(jnp.int32, (8, width), 0)
    return jnp.sum(jnp.where(lane == start + chan, wide, 0.0), axis=1, keepdims=True)


def long_work(blocks, scale, xu_ref, h_ref, vt_ref, gt_ref, o_ref, f_ref, t_ref, toep, stack, acc, v32, g32, gate, gp, fgs):
    cols = xu_ref.shape[2]
    me = lax.axis_index("seq")
    vt = [jnp.broadcast_to(column(vt_ref, j, me * 8), (8, cols)) for j in range(3)]
    gt = [jnp.broadcast_to(column(gt_ref, j, me * 8), (8, cols)) for j in range(3)]
    lane = lax.broadcasted_iota(jnp.int32, (8, cols), 1)
    sub_r = lax.broadcasted_iota(jnp.int32, (LANES, LANES), 0)
    sub_s = lax.broadcasted_iota(jnp.int32, (LANES, LANES), 1)
    full_r = lax.broadcasted_iota(jnp.int32, (cols, cols), 0)
    full_s = lax.broadcasted_iota(jnp.int32, (cols, cols), 1)
    flip = jnp.where(full_r + full_s == cols - 1, 1.0, 0.0).astype(BF16)

    def skew(block, half):
        row = h_ref[block, :, half * LANES : (half + 1) * LANES]
        return pltpu.roll(jnp.broadcast_to(row, (LANES, LANES)), 0, 1, stride=1, stride_axis=0)

    def build(block, carry):
        last_skew, last_edge = carry
        one, two = skew(block, 0), skew(block, 1)
        mid = jnp.where(sub_s >= sub_r, one, last_skew).astype(BF16)
        edge = jnp.where(sub_s >= sub_r, two, one).astype(BF16)
        toep[block, :LANES, :LANES] = mid
        toep[block, LANES:, LANES:] = mid
        toep[block, :LANES, LANES:] = edge
        toep[block, LANES:, :LANES] = last_edge
        return two, edge

    lax.fori_loop(
        0, blocks, build, (jnp.zeros((LANES, LANES), F32), jnp.zeros((LANES, LANES), BF16))
    )

    def short(block, carry):
        back1, back2 = carry
        both = xu_ref[block].astype(F32)
        x, u = both[:8], both[8:]
        roll1, roll2 = pltpu.roll(x, 1, 1), pltpu.roll(x, 2, 1)
        one = jnp.where(lane < 1, back1, roll1)
        two = jnp.where(lane < 2, back2, roll2)
        v32[block] = vt[0] * x + vt[1] * one + vt[2] * two
        g = gt[0] * x + gt[1] * one + gt[2] * two
        gate[block] = g
        g32[block] = g * u
        return roll1, roll2

    zero = jnp.zeros((8, cols), F32)
    lax.fori_loop(0, blocks, short, (zero, zero))

    rows = blocks * 8
    v16 = v32[...].reshape(rows, cols).astype(BF16)
    g16 = g32[...].reshape(rows, cols).astype(BF16)
    gp[0, :rows] = g16
    gp[0, rows:] = jnp.zeros((gp.shape[1] - rows, cols), BF16)
    gp[1, : rows - 16] = g32[1 : blocks - 1].reshape(rows - 16, cols).astype(BF16)
    gp[1, rows - 16 : rows] = jnp.concatenate([g32[blocks - 1], zero], axis=0).astype(BF16)
    gp[1, rows:] = jnp.zeros((gp.shape[1] - rows, cols), BF16)
    g32[...] = jnp.dot(g16, flip, preferred_element_type=F32).reshape(blocks, 8, cols)

    for shift in range(1, STACK):
        stack[:shift, :, shift * cols : (shift + 1) * cols] = jnp.zeros((shift, 16, cols), BF16)

    @pl.loop(0, blocks)
    def _(block):
        both = jnp.concatenate([v32[block], g32[blocks - 1 - block]], axis=0).astype(BF16)
        for shift in range(STACK):
            stack[block + shift, :, shift * cols : (shift + 1) * cols] = both

    for step in range(blocks // STACK):
        first = step * STACK
        left = stack[: blocks - first].reshape((blocks - first) * 16, STACK * cols)
        right = toep[first : first + STACK].reshape(STACK * cols, cols)
        part = jnp.dot(left, right, preferred_element_type=F32)
        part = part.reshape(blocks - first, 16, cols)
        if step == 0:
            acc[...] = part
        else:
            acc[first:] += part

    back = acc[:, 8:, :].reshape(rows, cols).astype(BF16)
    g32[...] = jnp.dot(back, flip, preferred_element_type=F32).reshape(blocks, 8, cols)

    def finish(step, carry):
        block = blocks - 1 - step
        nexts, sums = carry[:4], carry[4:]
        both = xu_ref[block].astype(F32)
        x, u = both[:8], both[8:]
        conv = acc[block, :8].astype(BF16).astype(F32)
        s0 = g32[step]
        c0 = (conv * u).astype(BF16).astype(F32)
        out = gate[block] * conv
        rolled = [pltpu.roll(s0, cols - 1, 1), pltpu.roll(s0, cols - 2, 1)]
        rolled += [pltpu.roll(c0, cols - 1, 1), pltpu.roll(c0, cols - 2, 1)]
        s1 = jnp.where(lane < cols - 1, rolled[0], nexts[0])
        s2 = jnp.where(lane < cols - 2, rolled[1], nexts[1])
        c1 = jnp.where(lane < cols - 1, rolled[2], nexts[2])
        c2 = jnp.where(lane < cols - 2, rolled[3], nexts[3])
        grad = vt[0] * s0 + vt[1] * s1 + vt[2] * s2 + (gt[0] * c0 + gt[1] * c1 + gt[2] * c2)
        o_ref[block] = jnp.concatenate([out, grad], axis=0).astype(BF16)
        terms = [s0, s1, s2, c0, c1, c2]
        return tuple(rolled) + tuple(a + t * x for a, t in zip(sums, terms))

    done = lax.fori_loop(0, blocks, finish, (zero,) * 10)
    spot = lax.broadcasted_iota(jnp.int32, (8, LANES), 1)
    chan = lax.broadcasted_iota(jnp.int32, (8, LANES), 0)
    row = jnp.zeros((8, LANES), F32)
    for j in range(6):
        total = jnp.sum(done[4 + j], axis=1, keepdims=True)
        row = jnp.where(spot == j * 8 + chan, jnp.broadcast_to(total, (8, LANES)), row)
    t_ref[...] = jnp.sum(row, axis=0, keepdims=True)

    v_flip = lax.dot_general(
        flip, v16, (((1,), (1,)), ((), ())), preferred_element_type=F32
    ).astype(BF16)
    upper = sub_r + sub_s >= LANES - 1

    def diagonal(tile):
        turned = pltpu.roll(tile, 1, 1, stride=1, stride_axis=0)
        return jnp.sum(turned, axis=0, keepdims=True) * scale

    def lag(depth, index, offset, parity, carry):
        last_mid, last_corner = carry
        right = gp[parity, pl.ds(pl.multiple_of(offset, 16), depth), :]
        prod = jnp.dot(v_flip[:, :depth], right, preferred_element_type=F32)
        edge = last_corner + prod[:LANES, :LANES]
        mid = prod[LANES:, :LANES] + prod[:LANES, LANES:]
        fgs[index, :, :LANES] = diagonal(jnp.where(upper, last_mid, edge))
        fgs[index, :, LANES:] = diagonal(jnp.where(upper, edge, mid))
        return mid, prod[LANES:, LANES:]

    def lags(depth, pair, carry):
        carry = lag(depth, 2 * pair, pair * 16, 0, carry)
        return lag(depth, 2 * pair + 1, pair * 16, 1, carry)

    carry = (jnp.zeros((LANES, LANES), F32),) * 2
    carry = lax.fori_loop(0, blocks // 4, partial(lags, rows), carry)
    carry = lax.fori_loop(blocks // 4, blocks // 2, partial(lags, rows // 2), carry)
    last_mid, last_corner = carry
    fgs[blocks, :, :LANES] = diagonal(jnp.where(upper, last_mid, last_corner))
    fgs[blocks, :, LANES:] = diagonal(jnp.where(upper, last_corner, 0.0))
    f_ref[...] = fgs[1:]


def exchange_out(
    blocks, replicas, o_ref, f_ref, t_ref, o_out, f_out, t_out,
    got, fx, fsum, fgot, tdp, trow, tgot, osem, orecv, xsem, fsem, frecv, dsem, drecv, tsem, trecv,
):
    me = lax.axis_index("seq")
    mine = lax.axis_index("dp")
    half = blocks // 2
    side = lax.rem(me, 2)
    sibling = me + 1 - 2 * side
    barrier = greet(blocks)

    @pl.loop(1, replicas)
    def _(step):
        peer = lax.rem(mine + step, replicas)
        pl.semaphore_signal(barrier, inc=1, device_id={"dp": peer}, device_id_type=MESH)

    raw = t_ref[...]
    lane = lax.broadcasted_iota(jnp.int32, (1, LANES), 1)
    squares = jnp.sum(jnp.where(lane < 48, raw * raw, 0.0), axis=1, keepdims=True)
    tdp[mine] = jnp.broadcast_to(squares, (1, LANES))
    got[me] = o_ref[me]
    pl.semaphore_wait(barrier, blocks + replicas - 2)

    def across(peer, source):
        return pltpu.make_async_remote_copy(
            src_ref=tdp.at[mine], dst_ref=tdp.at[source],
            send_sem=dsem.at[peer], recv_sem=drecv.at[source],
            device_id={"dp": peer}, device_id_type=MESH,
        )

    @pl.loop(1, replicas)
    def _(step):
        across(lax.rem(mine + step, replicas), mine).start()

    swap = pltpu.make_async_remote_copy(
        src_ref=f_ref.at[pl.ds((1 - side) * half, half)], dst_ref=fx,
        send_sem=xsem.at[0], recv_sem=xsem.at[1],
        device_id={"seq": sibling}, device_id_type=MESH,
    )
    swap.start()

    def main(peer, source):
        return pltpu.make_async_remote_copy(
            src_ref=o_ref.at[peer], dst_ref=got.at[source],
            send_sem=osem.at[peer], recv_sem=orecv.at[source],
            device_id={"seq": peer}, device_id_type=MESH,
        )

    @pl.loop(1, blocks)
    def _(step):
        main(lax.rem(me + step, blocks), me).start()

    @pl.loop(1, replicas)
    def _(step):
        peer = lax.rem(mine + step, replicas)
        across(peer, peer).wait_send()
        across(peer, peer).wait_recv()

    total = jnp.sum(tdp[...], axis=0)
    tgot[me] = jnp.where(lane < 48, raw, total)

    def around(peer, source):
        return pltpu.make_async_remote_copy(
            src_ref=tgot.at[me], dst_ref=tgot.at[source],
            send_sem=tsem.at[peer], recv_sem=trecv.at[source],
            device_id={"seq": peer}, device_id_type=MESH,
        )

    @pl.loop(1, blocks)
    def _(step):
        around(lax.rem(me + step, blocks), me).start()

    swap.wait()
    fsum[...] = f_ref[pl.ds(side * half, half)] + fx[...]

    def spread(index, peer, source):
        return pltpu.make_async_remote_copy(
            src_ref=fsum.at[index], dst_ref=fgot.at[source],
            send_sem=fsem.at[index], recv_sem=frecv.at[source],
            device_id={"seq": peer}, device_id_type=MESH,
        )

    home = me // half

    @pl.loop(0, half)
    def _(index):
        peer = side * half + index

        @pl.when(peer != me)
        def _():
            spread(index, peer, me // 2).start()

    @pl.when(home == side)
    def _():
        fgot[me // 2] = fsum[me - side * half]

    @pl.loop(0, half)
    def _(index):
        peer = side * half + index

        @pl.when(peer != me)
        def _():
            spread(index, peer, me // 2).wait_send()

        source = 2 * index + home

        @pl.when(source != me)
        def _():
            spread(index, peer, index).wait_recv()

    @pl.loop(1, blocks)
    def _(step):
        peer = lax.rem(me + step, blocks)
        main(peer, peer).wait_send()
        main(peer, peer).wait_recv()
        around(peer, peer).wait_send()
        around(peer, peer).wait_recv()

    o_out[...] = got[...]
    f_out[...] = fgot[...]
    t_out[...] = tgot[...]


def per_device(layer_in, cotangent, value_taps, gate_taps, long_filter):
    chans, cols = layer_in.shape
    blocks = lax.axis_size("seq")
    replicas = lax.axis_size("dp")
    half = blocks // 2
    scale = 1.0 / math.sqrt(GROUP * blocks * cols)
    vmem = pl.BlockSpec(memory_space=pltpu.VMEM)
    dma = pltpu.SemaphoreType.DMA
    both = jax.ShapeDtypeStruct((blocks, 16, cols), BF16)
    wide = jax.ShapeDtypeStruct((blocks, 1, cols), F32)
    xu, filt = pl.pallas_call(
        partial(exchange_in, blocks),
        out_shape=(both, wide),
        in_specs=[vmem] * 3,
        out_specs=(vmem, vmem),
        scratch_shapes=[
            pltpu.VMEM(both.shape, BF16),
            pltpu.VMEM(both.shape, BF16),
            pltpu.VMEM((half, 1, cols), F32),
            pltpu.VMEM(wide.shape, F32),
            dma((2, blocks)),
            dma((2, blocks)),
        ],
        compiler_params=pltpu.CompilerParams(
            collective_id=0, has_side_effects=True, vmem_limit_bytes=VMEM_LIMIT
        ),
        name="exchange_in",
    )(layer_in, cotangent, long_filter)
    out, filt_part, raw = pl.pallas_call(
        partial(long_work, blocks, scale),
        out_shape=(both, wide, jax.ShapeDtypeStruct((1, LANES), F32)),
        in_specs=[vmem] * 4,
        out_specs=(vmem,) * 3,
        scratch_shapes=[
            pltpu.VMEM((blocks, cols, cols), BF16),
            pltpu.VMEM((blocks + STACK, 16, STACK * cols), BF16),
            pltpu.VMEM((blocks, 16, cols), F32),
            pltpu.VMEM((blocks, 8, cols), F32),
            pltpu.VMEM((blocks, 8, cols), F32),
            pltpu.VMEM((blocks, 8, cols), F32),
            pltpu.VMEM((2, 2 * blocks * 8, cols), BF16),
            pltpu.VMEM((blocks + 1, 1, cols), F32),
        ],
        compiler_params=pltpu.CompilerParams(vmem_limit_bytes=VMEM_LIMIT),
        name="long_work",
    )(xu, filt, value_taps, gate_taps)
    got, filt_got, taps_got = pl.pallas_call(
        partial(exchange_out, blocks, replicas),
        out_shape=(
            both,
            jax.ShapeDtypeStruct((half, 1, cols), F32),
            jax.ShapeDtypeStruct((blocks, 1, LANES), F32),
        ),
        in_specs=[vmem] * 3,
        out_specs=(vmem,) * 3,
        scratch_shapes=[
            pltpu.VMEM(both.shape, BF16),
            pltpu.VMEM((half, 1, cols), F32),
            pltpu.VMEM((half, 1, cols), F32),
            pltpu.VMEM((half, 1, cols), F32),
            pltpu.VMEM((replicas, 1, LANES), F32),
            pltpu.VMEM((1, LANES), F32),
            pltpu.VMEM((blocks, 1, LANES), F32),
            dma((blocks,)),
            dma((blocks,)),
            dma((2,)),
            dma((half,)),
            dma((half,)),
            dma((replicas,)),
            dma((replicas,)),
            dma((blocks,)),
            dma((blocks,)),
        ],
        compiler_params=pltpu.CompilerParams(
            collective_id=1, has_side_effects=True, vmem_limit_bytes=VMEM_LIMIT
        ),
        name="exchange_out",
    )(out, filt_part, raw)
    parts = got.reshape(blocks, 2, 8, cols)
    layer_out = parts[:, 0].reshape(chans, cols)
    input_grad = parts[:, 1].reshape(chans, cols)
    rows = taps_got.reshape(blocks, LANES)
    total = jnp.sum(rows[:, 48])
    tap_scale = lax.rsqrt(total / F32(6 * chans * replicas) + 1e-05)
    taps = rows[:, :48].reshape(blocks, 6, 8).transpose(1, 0, 2).reshape(6, chans) * tap_scale
    return (layer_out, input_grad, taps[:3], taps[3:], filt_got.reshape(half, cols))


def solution(mesh):
    placed = (P("dp", "seq"), P("dp", "seq"), P(None, "dp"), P(None, "dp"), P("dp", "seq"))
    return jax.shard_map(
        per_device,
        mesh=mesh,
        in_specs=placed,
        out_specs=(P("dp", "seq"), P("dp", "seq"), P(None, "dp"), P(None, "dp"), P("dp", "seq")),
        check_vma=False,
    )
```

time: 722 us -> 132 us (0.18)
  the two profiles are of different devices: /device:TPU:0 before, /device:TPU:1 now
where the time goes in v1:
time: 132 us; the launch traced here: 131 us
  Pallas kernels  124 us (94%)
  local copies, waits for them, and re-layouts  5.75 us (4%)
  between operations  1.4 us (1%)
    pallas_call x1, Pallas kernels, per_device(): pl.pallas_call(partial(exchange_out, blocks, replicas), out_shape=(both,...  57.2 us
    pallas_call x1, Pallas kernels, per_device(): pl.pallas_call(partial(long_work, blocks, scale), out_shape=(both, wide,...  35.4 us
    pallas_call x1, Pallas kernels, per_device(): pl.pallas_call(partial(exchange_in, blocks), out_shape=(both, wide), in_s...  31 us
    unnamed x11, local copies, waits for them, and re-layouts  3.23 us

profile of v1, /device:TPU:1, one launch (start us, length us, event | category | flops | bytes accessed | tf_op | source)
XLA Modules:
  0.0 131.4 jit_solution(1509133974742603450)
XLA Ops:
  0.6 0.0 copy-start
  0.6 0.9 copy-done
  1.6 0.0 copy-start.1
  1.6 0.9 copy-done.1
  2.5 0.0 copy-start.2
  2.5 0.7 copy-done.2
  3.3 0.0 copy-start.3
  3.3 0.0 copy-start.4
  3.3 31.0 %exchange_in.1 = (bf16[64,16,256]{2,1,0:T(8,128)(2,1)S(1)}, f32[64,1,256]{2,1,0:T(1,128)S(1)}) custom-call(bf16[512,256]{1,0:T(8,128)(2,1)S(1)} %copy-done, bf16[512,256]{1,0:T(8,128)(2,1)S(1)} %copy-done.1, bf16[32,256]{1,0:T(8,128)(2,1)S(1)} %copy-done.2), custom_call_target="tpu_custom_call" | custom-call | tf_op jit(solution)/shard_map/exchange_in/pallas_call | solution.py:371
  34.3 0.0 copy-done.3
  34.3 0.0 copy-done.4
  34.3 35.4 %long_work.1 = (bf16[64,16,256]{2,1,0:T(8,128)(2,1)S(1)}, f32[64,1,256]{2,1,0:T(1,128)S(1)}, f32[1,128]{1,0:T(1,128)S(1)}) custom-call(bf16[64,16,256]{2,1,0:T(8,128)(2,1)S(1)} %get-tuple-element.13.xu_ref, f32[64,1,256]{2,1,0:T(1,128)S(1)} %get-tuple-element.14.h_ref, f32[3,512]{1,0:T(4,128)S(1)} %copy-done.3, f32[3,512]{1,0:T(4,128)S(1)} %copy-done.4), custom_call_target="tpu_custom_call" | custom-call | tf_op jit(solution)/shard_map/long_work/pallas_call | solution.py:389
  69.7 57.2 %exchange_out.1 = (bf16[64,16,256]{2,1,0:T(8,128)(2,1)S(1)}, f32[32,1,256]{2,1,0:T(1,128)S(1)}, f32[64,1,128]{2,1,0:T(1,128)S(1)}) custom-call(bf16[64,16,256]{2,1,0:T(8,128)(2,1)S(1)} %get-tuple-element.15.o_ref, f32[64,1,256]{2,1,0:T(1,128)S(1)} %get-tuple-element.16.f_ref, f32[1,128]{1,0:T(1,128)S(1)} %get-tuple-element.17.t_ref), custom_call_target="tpu_custom_call" | custom-call | tf_op jit(solution)/shard_map/exchange_out/pallas_call | solution.py:407
  126.9 0.7 slice_reduce_fusion
  128.3 0.1 copy.16
  128.3 0.8 slice_bitcast_fusion
  129.2 0.6 copy.21
  129.8 0.1 copy.18
  129.9 0.7 slice.31
  130.6 0.1 copy.17
  130.7 0.7 slice.29
  (2 shorter events, 0.0 us)
Async XLA Ops:
  0.6 1.0 copy-start
  1.6 0.9 copy-start.1
  2.5 0.7 copy-start.2
  3.3 31.0 %copy-start.3 = (f32[3,512]{1,0:T(4,128)S(1)}, f32[3,512]{1,0:T(4,128)}, u32[]{:S(2)}) copy-start(f32[3,512]{1,0:T(4,128)} %vt_ref.1) | copy-start | bytes 18436
  3.3 31.0 %copy-start.4 = (f32[3,512]{1,0:T(4,128)S(1)}, f32[3,512]{1,0:T(4,128)}, u32[]{:S(2)}) copy-start(f32[3,512]{1,0:T(4,128)} %gt_ref.1) | copy-start | bytes 18436

commit v2 on v0

v2 whole, which is shorter than its diff:
```python
from functools import partial
import math

import jax
import jax.numpy as jnp
from jax import lax
from jax.experimental import pallas as pl
from jax.experimental.pallas import tpu as pltpu
from jax.sharding import PartitionSpec as P

GROUP = 16
LANES = 128
STACK = 4
CHUNK = 8
MESH = pl.DeviceIdType.MESH
VMEM_LIMIT = 48 * 1024 * 1024
F32 = jnp.float32
BF16 = jnp.bfloat16


def widen(tile):
    wide = tile.astype(F32)
    return jnp.concatenate([wide[:, :8], wide[:, 8:]], axis=2)


def narrow(block):
    return jnp.concatenate([block[:, :, :LANES], block[:, :, LANES:]], axis=1).astype(BF16)


def to_messages(rows_ref, message_ref, blocks):
    @pl.loop(0, blocks // 2)
    def _(pair):
        rows = pl.ds(pl.multiple_of(pair * 16, 16), 16)
        wide = rows_ref[rows, :].astype(F32)
        message_ref[pl.ds(2 * pair, 2)] = narrow(wide.reshape(2, 8, 2 * LANES))


def from_messages(message_ref, rows_ref, blocks):
    @pl.loop(0, blocks // 2)
    def _(pair):
        rows = pl.ds(pl.multiple_of(pair * 16, 16), 16)
        wide = widen(message_ref[pl.ds(2 * pair, 2)])
        rows_ref[rows, :] = wide.reshape(16, 2 * LANES).astype(BF16)


def column(taps_ref, row, start):
    width = taps_ref.shape[1]
    wide = jnp.broadcast_to(taps_ref[row : row + 1, :], (8, width))
    lane = lax.broadcasted_iota(jnp.int32, (8, width), 1)
    chan = lax.broadcasted_iota(jnp.int32, (8, width), 0)
    return jnp.sum(jnp.where(lane == start + chan, wide, 0.0), axis=1, keepdims=True)


def fill_stack(load, stack, blocks, cols):
    for shift in range(2, STACK):
        stack[: shift // 2, :, shift * cols : (shift + 1) * cols] = jnp.zeros(
            (shift // 2, 16, cols), BF16
        )

    def body(pair, before):
        one, two = load(2 * pair), load(2 * pair + 1)
        even = jnp.concatenate([one, two], axis=0).astype(BF16)
        odd = jnp.concatenate([before, one], axis=0).astype(BF16)
        for shift in range(STACK):
            stack[pair + shift // 2, :, shift * cols : (shift + 1) * cols] = odd if shift % 2 else even
        return two

    lax.fori_loop(0, blocks // 2, body, jnp.zeros((8, cols), F32))


def long_conv(stack, toep, acc, blocks, cols):
    for step in range(blocks // STACK):
        first = step * STACK
        left = stack[: (blocks - first) // 2].reshape((blocks - first) * 8, STACK * cols)
        right = toep[first : first + STACK].reshape(STACK * cols, cols)
        part = jnp.dot(left, right, preferred_element_type=F32).reshape(blocks - first, 8, cols)
        if step == 0:
            acc[...] = part
        else:
            acc[first:] += part


def kernel(
    blocks, replicas, scale, norm,
    x_hbm, u_hbm, h_hbm, vt_hbm, gt_hbm,
    lo_out, ig_out, vt_out, gt_out, f_out,
    x_in, u_in, h_in, vt_ref, gt_ref,
    hpack, hgot, xpack, xgot, upack, ugot, lpack, lgot, ipack, igot,
    toep, stack, acc, v32, g32, gate, gp,
    fgs, fx, fsum, fgot, tdp, tgot, tall,
    loads, hsem, xsem, usem, lsem, isem, fsem, dsem, tsem,
):
    cols = x_hbm.shape[1]
    half = blocks // 2
    rows = blocks * 8
    me = lax.axis_index("seq")
    mine = lax.axis_index("dp")
    side = lax.rem(me, 2)
    chip = me // 2
    sibling = me + 1 - 2 * side

    barrier = pltpu.get_barrier_semaphore()

    @pl.loop(1, blocks)
    def _(step):
        peer = lax.rem(me + step, blocks)
        pl.semaphore_signal(barrier, inc=1, device_id={"seq": peer}, device_id_type=MESH)

    @pl.loop(1, replicas)
    def _(step):
        peer = lax.rem(mine + step, replicas)
        pl.semaphore_signal(barrier, inc=1, device_id={"dp": peer}, device_id_type=MESH)

    pairs = ((h_hbm, h_in), (x_hbm, x_in), (u_hbm, u_in), (vt_hbm, vt_ref), (gt_hbm, gt_ref))
    fetched = [pltpu.make_async_copy(a, b, loads.at[i]) for i, (a, b) in enumerate(pairs)]
    for copy in fetched:
        copy.start()

    def to_seq(source, target, sems, peer):
        return pltpu.make_async_remote_copy(
            src_ref=source, dst_ref=target, send_sem=sems.at[0], recv_sem=sems.at[1],
            device_id={"seq": peer}, device_id_type=MESH,
        )

    def send_all(pack, got, sems):
        @pl.loop(1, blocks)
        def _(step):
            peer = lax.rem(me + step, blocks)
            to_seq(pack.at[peer], got.at[me], sems, peer).start()

    def drain(ref, count, sem):
        part = ref.at[pl.ds(0, count)]
        pltpu.make_async_copy(part, part, sem).wait()

    fetched[0].wait()
    taps = h_in[...].astype(F32)
    for row in range(half):
        hpack[row] = taps[row : row + 1]
    hgot[side, chip] = hpack[chip]
    fetched[1].wait()
    to_messages(x_in, xpack, blocks)
    xgot[me] = xpack[me]
    fetched[2].wait()
    to_messages(u_in, upack, blocks)
    ugot[me] = upack[me]
    pl.semaphore_wait(barrier, blocks + replicas - 2)

    @pl.loop(1, half)
    def _(step):
        there = lax.rem(chip + step, half)
        to_seq(hpack.at[there], hgot.at[side, chip], hsem.at[0], 2 * there + side).start()

    send_all(xpack, xgot, xsem)
    drain(hgot.at[side], half - 1, hsem.at[0, 1])
    swap_h = to_seq(hgot.at[side], hgot.at[side], hsem.at[1], sibling)
    swap_h.start()
    send_all(upack, ugot, usem)

    fetched[3].wait()
    fetched[4].wait()
    vt = [jnp.broadcast_to(column(vt_ref, j, me * 8), (8, cols))[None] for j in range(3)]
    gt = [jnp.broadcast_to(column(gt_ref, j, me * 8), (8, cols))[None] for j in range(3)]
    lane = lax.broadcasted_iota(jnp.int32, (CHUNK, 8, cols), 2)
    sub_r = lax.broadcasted_iota(jnp.int32, (LANES, LANES), 0)
    sub_s = lax.broadcasted_iota(jnp.int32, (LANES, LANES), 1)
    full_r = lax.broadcasted_iota(jnp.int32, (cols, cols), 0)
    full_s = lax.broadcasted_iota(jnp.int32, (cols, cols), 1)
    flip = jnp.where(full_r + full_s == cols - 1, 1.0, 0.0).astype(BF16)
    zero = jnp.zeros((1, 8, cols), F32)
    swap_h.wait()

    def skew(block, part):
        row = hgot[lax.rem(block, 2), block // 2, :, part * LANES : (part + 1) * LANES]
        return pltpu.roll(jnp.broadcast_to(row, (LANES, LANES)), 0, 1, stride=1, stride_axis=0)

    def build(block, carry):
        last_skew, last_edge = carry
        one, two = skew(block, 0), skew(block, 1)
        mid = jnp.where(sub_s >= sub_r, one, last_skew).astype(BF16)
        edge = jnp.where(sub_s >= sub_r, two, one).astype(BF16)
        toep[block, :LANES, :LANES] = mid
        toep[block, LANES:, LANES:] = mid
        toep[block, :LANES, LANES:] = edge
        toep[block, LANES:, :LANES] = last_edge
        return two, edge

    lax.fori_loop(
        0, blocks, build, (jnp.zeros((LANES, LANES), F32), jnp.zeros((LANES, LANES), BF16))
    )

    drain(xgot, blocks - 1, xsem.at[1])

    def short(chunk, carry):
        part = pl.ds(chunk * CHUNK, CHUNK)
        x = widen(xgot[part])
        roll1, roll2 = pltpu.roll(x, 1, 2), pltpu.roll(x, 2, 2)
        one = jnp.where(lane < 1, jnp.concatenate([carry[0], roll1[:-1]], axis=0), roll1)
        two = jnp.where(lane < 2, jnp.concatenate([carry[1], roll2[:-1]], axis=0), roll2)
        v32[part] = vt[0] * x + vt[1] * one + vt[2] * two
        gate[part] = gt[0] * x + gt[1] * one + gt[2] * two
        return roll1[-1:], roll2[-1:]

    lax.fori_loop(0, blocks // CHUNK, short, (zero, zero))
    fill_stack(lambda block: v32[block], stack, blocks, cols)
    long_conv(stack, toep, acc, blocks, cols)

    @pl.loop(0, blocks // CHUNK)
    def _(chunk):
        part = pl.ds(chunk * CHUNK, CHUNK)
        conv = acc[part].astype(BF16).astype(F32)
        acc[part] = conv
        lpack[part] = narrow(gate[part] * conv)

    lgot[me] = lpack[me]
    send_all(lpack, lgot, lsem)

    drain(ugot, blocks - 1, usem.at[1])

    @pl.loop(0, blocks // CHUNK)
    def _(chunk):
        part = pl.ds(chunk * CHUNK, CHUNK)
        u = widen(ugot[part])
        g32[part] = gate[part] * u
        gate[part] = (acc[part] * u).astype(BF16).astype(F32)

    g16 = g32[...].reshape(rows, cols).astype(BF16)
    gp[0, :rows] = g16
    gp[0, rows:] = jnp.zeros((gp.shape[1] - rows, cols), BF16)
    gp[1, : rows - 16] = g32[1 : blocks - 1].reshape(rows - 16, cols).astype(BF16)
    gp[1, rows - 16 : rows] = jnp.concatenate(
        [g32[blocks - 1], jnp.zeros((8, cols), F32)], axis=0
    ).astype(BF16)
    gp[1, rows:] = jnp.zeros((gp.shape[1] - rows, cols), BF16)
    g32[...] = jnp.dot(g16, flip, preferred_element_type=F32).reshape(blocks, 8, cols)
    fill_stack(lambda block: g32[blocks - 1 - block], stack, blocks, cols)
    long_conv(stack, toep, acc, blocks, cols)
    back = acc[...].reshape(rows, cols).astype(BF16)
    g32[...] = jnp.dot(back, flip, preferred_element_type=F32).reshape(blocks, 8, cols)

    def finish(step, carry):
        first = (blocks // CHUNK - 1 - step) * CHUNK
        part = pl.ds(first, CHUNK)
        x = widen(xgot[part])
        s0 = jnp.concatenate(
            [g32[blocks - 1 - first - i][None] for i in range(CHUNK)], axis=0
        )
        c0 = gate[part]

        def ahead(wide, shift, after):
            turned = pltpu.roll(wide, cols - shift, 2)
            later = jnp.concatenate([turned[1:], after], axis=0)
            return jnp.where(lane < cols - shift, turned, later), turned[:1]

        s1, n0 = ahead(s0, 1, carry[0])
        s2, n1 = ahead(s0, 2, carry[1])
        c1, n2 = ahead(c0, 1, carry[2])
        c2, n3 = ahead(c0, 2, carry[3])
        grad = vt[0] * s0 + vt[1] * s1 + vt[2] * s2 + (gt[0] * c0 + gt[1] * c1 + gt[2] * c2)
        ipack[part] = narrow(grad)
        terms = [jnp.sum(t * x, axis=0, keepdims=True) for t in (s0, s1, s2, c0, c1, c2)]
        return (n0, n1, n2, n3) + tuple(a + t for a, t in zip(carry[4:], terms))

    done = lax.fori_loop(0, blocks // CHUNK, finish, (zero,) * 10)
    igot[me] = ipack[me]
    send_all(ipack, igot, isem)

    spot = lax.broadcasted_iota(jnp.int32, (8, LANES), 1)
    chan = lax.broadcasted_iota(jnp.int32, (8, LANES), 0)
    row = jnp.zeros((8, LANES), F32)
    for j in range(6):
        total = jnp.sum(done[4 + j][0], axis=1, keepdims=True)
        row = jnp.where(spot == j * 8 + chan, jnp.broadcast_to(total, (8, LANES)), row)
    raw = jnp.sum(row, axis=0, keepdims=True)
    squares = jnp.sum(raw * raw, axis=1, keepdims=True)
    tdp[mine] = jnp.broadcast_to(squares, (1, LANES))

    @pl.loop(1, replicas)
    def _(step):
        peer = lax.rem(mine + step, replicas)
        pltpu.make_async_remote_copy(
            src_ref=tdp.at[mine], dst_ref=tdp.at[mine], send_sem=dsem.at[0], recv_sem=dsem.at[1],
            device_id={"dp": peer}, device_id_type=MESH,
        ).start()

    v16 = v32[...].reshape(rows, cols).astype(BF16)
    v_flip = lax.dot_general(
        flip, v16, (((1,), (1,)), ((), ())), preferred_element_type=F32
    ).astype(BF16)
    upper = sub_r + sub_s >= LANES - 1

    def diagonal(tile):
        turned = pltpu.roll(tile, 1, 1, stride=1, stride_axis=0)
        return jnp.sum(turned, axis=0, keepdims=True) * scale

    def lag(depth, parity, pair, carry):
        last_mid, last_corner = carry
        right = gp[parity, pl.ds(pl.multiple_of(pair * 16, 16), depth), :]
        prod = jnp.dot(v_flip[:, :depth], right, preferred_element_type=F32)
        edge = last_corner + prod[:LANES, :LANES]
        mid = prod[LANES:, :LANES] + prod[:LANES, LANES:]
        index = pair if parity else pair
        fgs[parity, index, :, :LANES] = diagonal(jnp.where(upper, last_mid, edge))
        fgs[parity, index, :, LANES:] = diagonal(jnp.where(upper, edge, mid))
        return mid, prod[LANES:, LANES:]

    def lags(depth, pair, carry):
        return lag(depth, 1, pair, lag(depth, 0, pair, carry))

    carry = (jnp.zeros((LANES, LANES), F32),) * 2
    carry = lax.fori_loop(0, blocks // 4, partial(lags, rows), carry)
    carry = lax.fori_loop(blocks // 4, half, partial(lags, rows // 2), carry)
    last_mid, last_corner = carry
    fgs[0, half, :, :LANES] = diagonal(jnp.where(upper, last_mid, last_corner))
    fgs[0, half, :, LANES:] = diagonal(jnp.where(upper, last_corner, 0.0))

    swap_f = to_seq(fgs.at[side, pl.ds(1 - side, half)], fx, fsem.at[0], sibling)
    swap_f.start()

    drain(tdp, replicas - 1, dsem.at[0])
    drain(tdp, replicas - 1, dsem.at[1])
    total = tdp[0]
    for other in range(1, replicas):
        total = total + tdp[other]
    spot_row = lax.broadcasted_iota(jnp.int32, (1, LANES), 1)
    tgot[me] = jnp.where(spot_row < 48, raw, total)

    @pl.loop(1, blocks)
    def _(step):
        peer = lax.rem(me + step, blocks)
        to_seq(tgot.at[me], tgot.at[me], tsem, peer).start()

    swap_f.wait()
    fsum[...] = fgs[1 - side, pl.ds(side, half)] + fx[...]
    fgot[chip] = fsum[chip]

    @pl.loop(1, half)
    def _(step):
        there = lax.rem(chip + step, half)
        to_seq(fsum.at[there], fgot.at[chip], fsem.at[1], 2 * there + side).start()

    drain(lgot, blocks - 1, lsem.at[1])
    from_messages(lgot, lo_out, blocks)

    drain(tgot, blocks - 1, tsem.at[1])
    for block in range(blocks):
        tall[block : block + 1, :] = tgot[block]
    every = tall[...]
    total = jnp.sum(every[:, 48:49], axis=0, keepdims=True)
    factor = lax.rsqrt(total * norm + 1e-05)
    width = blocks * 8
    pick_k = lax.broadcasted_iota(jnp.int32, (LANES, width), 0)
    pick_l = lax.broadcasted_iota(jnp.int32, (LANES, width), 1)
    own_i = lax.broadcasted_iota(jnp.int32, (blocks, width), 0)
    own_l = lax.broadcasted_iota(jnp.int32, (blocks, width), 1)
    for j in range(6):
        pick = jnp.where(pick_k == 8 * j + lax.rem(pick_l, 8), 1.0, 0.0)
        spread = jnp.dot(every, pick, precision=lax.Precision.HIGHEST, preferred_element_type=F32)
        line = jnp.sum(jnp.where(own_i == own_l // 8, spread, 0.0), axis=0, keepdims=True)
        (gt_out if j >= 3 else vt_out)[j % 3 : j % 3 + 1, :] = line * factor

    drain(fgot, half - 1, fsem.at[1, 1])
    for block in range(half):
        f_out[block : block + 1, :] = fgot[block]
    drain(igot, blocks - 1, isem.at[1])
    from_messages(igot, ig_out, blocks)

    for ref, sems in ((xpack, xsem), (upack, usem), (lpack, lsem), (ipack, isem), (tgot, tsem)):
        drain(ref, blocks - 1, sems.at[0])
    drain(hpack, half - 1, hsem.at[0, 0])
    drain(fsum, half - 1, fsem.at[1, 0])


def per_device(layer_in, cotangent, value_taps, gate_taps, long_filter):
    chans, cols = layer_in.shape
    blocks = lax.axis_size("seq")
    replicas = lax.axis_size("dp")
    half = blocks // 2
    scale = 1.0 / math.sqrt(GROUP * blocks * cols)
    norm = 1.0 / (6 * chans * replicas)
    vmem = pl.BlockSpec(memory_space=pltpu.VMEM)
    anywhere = pl.BlockSpec(memory_space=pl.ANY)
    dma = pltpu.SemaphoreType.DMA
    message = pltpu.VMEM((blocks, 16, LANES), BF16)
    wide = pltpu.VMEM((blocks, 8, cols), F32)
    lines = pltpu.VMEM((half, 1, cols), F32)
    outs = pl.pallas_call(
        partial(kernel, blocks, replicas, scale, norm),
        out_shape=(
            jax.ShapeDtypeStruct((chans, cols), BF16),
            jax.ShapeDtypeStruct((chans, cols), BF16),
            jax.ShapeDtypeStruct((3, chans), F32),
            jax.ShapeDtypeStruct((3, chans), F32),
            jax.ShapeDtypeStruct((half, cols), F32),
        ),
        in_specs=[anywhere] * 5,
        out_specs=(vmem,) * 5,
        scratch_shapes=[
            pltpu.VMEM((chans, cols), BF16),
            pltpu.VMEM((chans, cols), BF16),
            pltpu.VMEM((half, cols), BF16),
            pltpu.VMEM((3, chans), F32),
            pltpu.VMEM((3, chans), F32),
            lines,
            pltpu.VMEM((2, half, 1, cols), F32),
            *([message] * 8),
            pltpu.VMEM((blocks, cols, cols), BF16),
            pltpu.VMEM((half + STACK // 2, 16, STACK * cols), BF16),
            *([wide] * 4),
            pltpu.VMEM((2, 2 * blocks * 8, cols), BF16),
            pltpu.VMEM((2, half + 1, 1, cols), F32),
            lines,
            lines,
            lines,
            pltpu.VMEM((replicas, 1, LANES), F32),
            pltpu.VMEM((blocks, 1, LANES), F32),
            pltpu.VMEM((blocks, LANES), F32),
            dma((5,)),
            dma((2, 2)),
            dma((2,)),
            dma((2,)),
            dma((2,)),
            dma((2,)),
            dma((2, 2)),
            dma((2,)),
            dma((2,)),
        ],
        compiler_params=pltpu.CompilerParams(
            collective_id=0, has_side_effects=True, vmem_limit_bytes=VMEM_LIMIT
        ),
        name="hyena",
    )(layer_in, cotangent, long_filter, value_taps, gate_taps)
    return outs


def solution(mesh):
    placed = (P("dp", "seq"), P("dp", "seq"), P(None, "dp"), P(None, "dp"), P("dp", "seq"))
    return jax.shard_map(
        per_device,
        mesh=mesh,
        in_specs=placed,
        out_specs=(P("dp", "seq"), P("dp", "seq"), P(None, "dp"), P(None, "dp"), P("dp", "seq")),
        check_vma=False,
    )
```

time: 722 us -> 88.2 us (0.12)
  the two profiles are of different devices: /device:TPU:0 before, /device:TPU:1 now
where the time goes in v2:
time: 88.2 us; the launch traced here: 87.8 us
  Pallas kernels  80 us (91%)
  local copies, waits for them, and re-layouts  7.22 us (8%)
    pallas_call x1, Pallas kernels, per_device(): pl.pallas_call(partial(kernel, blocks, replicas, scale, norm), out_shape=...  80 us
    unnamed x15, local copies, waits for them, and re-layouts  7.22 us

profile of v2, /device:TPU:1, one launch (start us, length us, event | category | flops | bytes accessed | tf_op | source)
XLA Modules:
  0.0 87.8 jit_solution(4360232215023675504)
XLA Ops:
  0.6 0.0 copy-start
  0.6 0.9 %copy-done = bf16[512,256]{1,0:T(8,128)(2,1)S(1)} copy-done((bf16[512,256]{1,0:T(8,128)(2,1)S(1)}, bf16[512,256]{1,0:T(8,128)(2,1)}, u32[]{:S(2)}) %copy-start) | copy-done | bytes 262168
  1.6 0.0 copy-start.1
  1.6 0.9 %copy-done.1 = bf16[512,256]{1,0:T(8,128)(2,1)S(1)} copy-done((bf16[512,256]{1,0:T(8,128)(2,1)S(1)}, bf16[512,256]{1,0:T(8,128)(2,1)}, u32[]{:S(2)}) %copy-start.1) | copy-done | bytes 262168
  2.5 0.0 copy-start.2
  2.5 0.7 copy-done.2
  3.3 0.0 copy-start.3
  3.3 0.7 copy-done.3
  3.9 0.0 copy-start.4
  4.0 0.7 copy-done.4
  4.6 80.0 %hyena.1 = (bf16[512,256]{1,0:T(8,128)(2,1)S(1)}, bf16[512,256]{1,0:T(8,128)(2,1)S(1)}, f32[3,512]{1,0:T(4,128)S(1)}, f32[3,512]{1,0:T(4,128)S(1)}, f32[32,256]{1,0:T(8,128)S(1)}) custom-call(bf16[512,256]{1,0:T(8,128)(2,1)S(1)} %copy-done, bf16[512,256]{1,0:T(8,128)(2,1)S(1)} %copy-done.1, bf16[32,256]{1,0:T(8,128)(2,1)S(1)} %copy-done.2, ...), custom_call_target="tpu_custom_call" | custom-call | tf_op jit(solution)/shard_map/hyena/pallas_call | solution.py:386
  84.6 0.7 copy.15
  85.3 0.7 copy.16
  86.0 0.6 copy.17
  86.6 0.6 copy.18
  87.2 0.6 copy.19
Async XLA Ops:
  0.6 1.0 %copy-start = (bf16[512,256]{1,0:T(8,128)(2,1)S(1)}, bf16[512,256]{1,0:T(8,128)(2,1)}, u32[]{:S(2)}) copy-start(bf16[512,256]{1,0:T(8,128)(2,1)} %x_hbm.1) | copy-start | bytes 786436
  1.6 0.9 %copy-start.1 = (bf16[512,256]{1,0:T(8,128)(2,1)S(1)}, bf16[512,256]{1,0:T(8,128)(2,1)}, u32[]{:S(2)}) copy-start(bf16[512,256]{1,0:T(8,128)(2,1)} %u_hbm.1) | copy-start | bytes 786436
  2.5 0.7 copy-start.2
  3.3 0.7 copy-start.3
  3.9 0.7 copy-start.4

commit v3 on v2

v3 whole, which is shorter than its diff:
```python
from functools import partial
import math

import jax
import jax.numpy as jnp
from jax import lax
from jax.experimental import pallas as pl
from jax.experimental.pallas import tpu as pltpu
from jax.sharding import PartitionSpec as P

GROUP = 16
LANES = 128
STACK = 8
CHUNK = 8
UNROLL = 4
TURNS = 2
PART = 40
MESH = pl.DeviceIdType.MESH
VMEM_LIMIT = 60 * 1024 * 1024
F32 = jnp.float32
BF16 = jnp.bfloat16


def widen(tile):
    wide = tile.astype(F32)
    return jnp.concatenate([wide[:, :8], wide[:, 8:]], axis=2)


def narrow(block):
    return jnp.concatenate([block[:, :, :LANES], block[:, :, LANES:]], axis=1).astype(BF16)


def to_messages(rows_ref, message_ref, blocks):
    @pl.loop(0, blocks // 2)
    def _(pair):
        rows = pl.ds(pl.multiple_of(pair * 16, 16), 16)
        wide = rows_ref[rows, :].astype(F32)
        message_ref[pl.ds(2 * pair, 2)] = narrow(wide.reshape(2, 8, 2 * LANES))


def from_messages(message_ref, rows_ref, blocks):
    @pl.loop(0, blocks // 2)
    def _(pair):
        rows = pl.ds(pl.multiple_of(pair * 16, 16), 16)
        wide = widen(message_ref[pl.ds(2 * pair, 2)])
        rows_ref[rows, :] = wide.reshape(16, 2 * LANES).astype(BF16)


def column(taps_ref, row, start):
    width = taps_ref.shape[1]
    wide = jnp.broadcast_to(taps_ref[row : row + 1, :], (8, width))
    lane = lax.broadcasted_iota(jnp.int32, (8, width), 1)
    chan = lax.broadcasted_iota(jnp.int32, (8, width), 0)
    return jnp.sum(jnp.where(lane == start + chan, wide, 0.0), axis=1, keepdims=True)


def fill_stack(load, stack, blocks, cols):
    for shift in range(2, STACK):
        stack[: shift // 2, :, shift * cols : (shift + 1) * cols] = jnp.zeros(
            (shift // 2, 16, cols), BF16
        )

    def body(pair, before):
        one, two = load(2 * pair), load(2 * pair + 1)
        even = jnp.concatenate([one, two], axis=0).astype(BF16)
        odd = jnp.concatenate([before, one], axis=0).astype(BF16)
        for shift in range(STACK):
            stack[pair + shift // 2, :, shift * cols : (shift + 1) * cols] = odd if shift % 2 else even
        return two

    lax.fori_loop(0, blocks // 2, body, jnp.zeros((8, cols), F32))


def long_conv(stack, toep, acc, blocks, cols):
    turns = blocks // STACK
    acc[...] = jnp.zeros(acc.shape, F32)
    for start in range(0, turns, TURNS):
        depth = blocks - start * STACK
        left = stack[: depth // 2].reshape(depth * 8, STACK * cols)

        @pl.loop(start, start + TURNS)
        def _(turn):
            first = turn * STACK
            right = toep[pl.ds(first, STACK)].reshape(STACK * cols, cols)
            part = jnp.dot(left, right, preferred_element_type=F32).reshape(depth, 8, cols)
            acc[pl.ds(first, depth)] += part


def kernel(
    blocks, replicas, scale, norm,
    x_hbm, u_hbm, h_hbm, vt_hbm, gt_hbm,
    lgot, igot, fgot, t_out,
    x_in, u_in, h_in, vt_ref, gt_ref,
    hpack, hgot, xpack, xgot, upack, ugot, lpack, ipack,
    toep, stack, acc, v32, g32, r32, gate, gp,
    fgs, fx, fsum, twin, tdp, tnorm, tgot, tall, t_vmem,
    loads, hsem, xsem, usem, lsem, isem, fsem, dsem, tsem, own,
):
    cols = x_hbm.shape[1]
    half = blocks // 2
    rows = blocks * 8
    me = lax.axis_index("seq")
    mine = lax.axis_index("dp")
    side = lax.rem(me, 2)
    chip = me // 2
    sibling = me + 1 - 2 * side

    barrier = pltpu.get_barrier_semaphore()

    @pl.loop(1, blocks)
    def _(step):
        peer = lax.rem(me + step, blocks)
        pl.semaphore_signal(barrier, inc=1, device_id={"seq": peer}, device_id_type=MESH)

    lead = half

    @pl.when(me == lead)
    def _():
        @pl.loop(1, replicas)
        def _(step):
            peer = lax.rem(mine + step, replicas)
            pl.semaphore_signal(barrier, inc=1, device_id={"dp": peer}, device_id_type=MESH)

    pairs = ((h_hbm, h_in), (x_hbm, x_in), (u_hbm, u_in), (vt_hbm, vt_ref), (gt_hbm, gt_ref))
    fetched = [pltpu.make_async_copy(a, b, loads.at[i]) for i, (a, b) in enumerate(pairs)]
    for copy in fetched:
        copy.start()

    def to_seq(source, target, sems, peer):
        return pltpu.make_async_remote_copy(
            src_ref=source, dst_ref=target, send_sem=sems.at[0], recv_sem=sems.at[1],
            device_id={"seq": peer}, device_id_type=MESH,
        )

    def send_some(pack, got, sems, first, last):
        @pl.loop(first, last)
        def _(step):
            peer = lax.rem(me + step, blocks)
            to_seq(pack.at[peer], got.at[me], sems, peer).start()

    def drain(ref, count, sem):
        part = ref.at[pl.ds(0, count)]
        pltpu.make_async_copy(part, part, sem).wait()

    fetched[0].wait()
    taps = h_in[...].astype(F32)
    for row in range(half):
        hpack[row] = taps[row : row + 1]
    hgot[side, chip] = hpack[chip]
    fetched[1].wait()
    to_messages(x_in, xpack, blocks)
    xgot[me] = xpack[me]
    fetched[2].wait()
    to_messages(u_in, upack, blocks)
    ugot[me] = upack[me]
    pl.semaphore_wait(barrier, blocks - 1 + jnp.where(me == lead, replicas - 1, 0))

    @pl.loop(1, half)
    def _(step):
        there = lax.rem(chip + step, half)
        to_seq(hpack.at[there], hgot.at[side, chip], hsem.at[0], 2 * there + side).start()

    send_some(xpack, xgot, xsem, 1, blocks)
    drain(hgot.at[side], half - 1, hsem.at[0, 1])
    swap_h = to_seq(hgot.at[side], hgot.at[side], hsem.at[1], sibling)
    swap_h.start()
    send_some(upack, ugot, usem, 1, blocks)

    fetched[3].wait()
    fetched[4].wait()
    vt = [jnp.broadcast_to(column(vt_ref, j, me * 8), (8, cols))[None] for j in range(3)]
    gt = [jnp.broadcast_to(column(gt_ref, j, me * 8), (8, cols))[None] for j in range(3)]
    lane = lax.broadcasted_iota(jnp.int32, (CHUNK, 8, cols), 2)
    sub_r = lax.broadcasted_iota(jnp.int32, (LANES, LANES), 0)
    sub_s = lax.broadcasted_iota(jnp.int32, (LANES, LANES), 1)
    full_r = lax.broadcasted_iota(jnp.int32, (cols, cols), 0)
    full_s = lax.broadcasted_iota(jnp.int32, (cols, cols), 1)
    flip = jnp.where(full_r + full_s == cols - 1, 1.0, 0.0).astype(BF16)
    zero = jnp.zeros((1, 8, cols), F32)
    swap_h.wait()

    def skew(block, part):
        row = hgot[lax.rem(block, 2), block // 2, :, part * LANES : (part + 1) * LANES]
        return pltpu.roll(jnp.broadcast_to(row, (LANES, LANES)), 0, 1, stride=1, stride_axis=0)

    def build(group, carry):
        last_skew, last_edge = carry
        for i in range(UNROLL):
            block = group * UNROLL + i
            one, two = skew(block, 0), skew(block, 1)
            mid = jnp.where(sub_s >= sub_r, one, last_skew).astype(BF16)
            edge = jnp.where(sub_s >= sub_r, two, one).astype(BF16)
            toep[block, :LANES, :LANES] = mid
            toep[block, LANES:, LANES:] = mid
            toep[block, :LANES, LANES:] = edge
            toep[block, LANES:, :LANES] = last_edge
            last_skew, last_edge = two, edge
        return last_skew, last_edge

    lax.fori_loop(
        0,
        blocks // UNROLL,
        build,
        (jnp.zeros((LANES, LANES), F32), jnp.zeros((LANES, LANES), BF16)),
    )

    drain(xgot, blocks - 1, xsem.at[1])

    def short(chunk, carry):
        part = pl.ds(chunk * CHUNK, CHUNK)
        x = widen(xgot[part])
        roll1, roll2 = pltpu.roll(x, 1, 2), pltpu.roll(x, 2, 2)
        one = jnp.where(lane < 1, jnp.concatenate([carry[0], roll1[:-1]], axis=0), roll1)
        two = jnp.where(lane < 2, jnp.concatenate([carry[1], roll2[:-1]], axis=0), roll2)
        v32[part] = vt[0] * x + vt[1] * one + vt[2] * two
        gate[part] = gt[0] * x + gt[1] * one + gt[2] * two
        return roll1[-1:], roll2[-1:]

    lax.fori_loop(0, blocks // CHUNK, short, (zero, zero))
    fill_stack(lambda block: v32[block], stack, blocks, cols)
    long_conv(stack, toep, acc, blocks, cols)

    @pl.loop(0, blocks // CHUNK)
    def _(chunk):
        part = pl.ds(chunk * CHUNK, CHUNK)
        conv = acc[part].astype(BF16).astype(F32)
        acc[part] = conv
        lpack[part] = narrow(gate[part] * conv)

    keep_l = pltpu.make_async_copy(lpack.at[me], lgot.at[me], own.at[0])
    keep_l.start()
    send_some(lpack, lgot, lsem, 1, blocks)

    drain(ugot, blocks - 1, usem.at[1])

    @pl.loop(0, blocks // CHUNK)
    def _(chunk):
        part = pl.ds(chunk * CHUNK, CHUNK)
        u = widen(ugot[part])
        g32[part] = gate[part] * u
        gate[part] = (acc[part] * u).astype(BF16).astype(F32)

    g16 = g32[...].reshape(rows, cols).astype(BF16)
    r32[...] = jnp.dot(g16, flip, preferred_element_type=F32).reshape(blocks, 8, cols)
    fill_stack(lambda block: r32[blocks - 1 - block], stack, blocks, cols)
    long_conv(stack, toep, acc, blocks, cols)
    back = acc[:blocks].reshape(rows, cols).astype(BF16)
    r32[...] = jnp.dot(back, flip, preferred_element_type=F32).reshape(blocks, 8, cols)

    def finish(step, carry):
        first = (blocks // CHUNK - 1 - step) * CHUNK
        part = pl.ds(first, CHUNK)
        x = widen(xgot[part])
        s0 = jnp.concatenate(
            [r32[blocks - 1 - first - i][None] for i in range(CHUNK)], axis=0
        )
        c0 = gate[part]

        def ahead(wide, shift, after):
            turned = pltpu.roll(wide, cols - shift, 2)
            later = jnp.concatenate([turned[1:], after], axis=0)
            return jnp.where(lane < cols - shift, turned, later), turned[:1]

        s1, n0 = ahead(s0, 1, carry[0])
        s2, n1 = ahead(s0, 2, carry[1])
        c1, n2 = ahead(c0, 1, carry[2])
        c2, n3 = ahead(c0, 2, carry[3])
        grad = vt[0] * s0 + vt[1] * s1 + vt[2] * s2 + (gt[0] * c0 + gt[1] * c1 + gt[2] * c2)
        ipack[part] = narrow(grad)
        terms = [jnp.sum(t * x, axis=0, keepdims=True) for t in (s0, s1, s2, c0, c1, c2)]
        return (n0, n1, n2, n3) + tuple(a + t for a, t in zip(carry[4:], terms))

    done = lax.fori_loop(0, blocks // CHUNK, finish, (zero,) * 10)
    spot = lax.broadcasted_iota(jnp.int32, (8, LANES), 1)
    chan = lax.broadcasted_iota(jnp.int32, (8, LANES), 0)
    row = jnp.zeros((8, LANES), F32)
    for j in range(6):
        total = jnp.sum(done[4 + j][0], axis=1, keepdims=True)
        row = jnp.where(
            spot == side * 48 + j * 8 + chan, jnp.broadcast_to(total, (8, LANES)), row
        )
    twin[side] = jnp.sum(row, axis=0, keepdims=True)
    swap_t = to_seq(twin.at[side], twin.at[side], tsem.at[1], sibling)
    swap_t.start()
    keep_i = pltpu.make_async_copy(ipack.at[me], igot.at[me], own.at[1])
    keep_i.start()
    send_some(ipack, igot, isem, 1, 8)
    swap_t.wait()
    raw = twin[0] + twin[1]
    tgot[chip] = raw

    @pl.loop(1, half)
    def _(step):
        there = lax.rem(chip + step, half)
        to_seq(tgot.at[chip], tgot.at[chip], tsem.at[0], 2 * there + side).start()

    send_some(ipack, igot, isem, 8, PART)

    gp[0, :rows] = g16
    gp[0, rows:] = jnp.zeros((gp.shape[1] - rows, cols), BF16)
    gp[1, : rows - 16] = g32[1 : blocks - 1].reshape(rows - 16, cols).astype(BF16)
    gp[1, rows - 16 : rows] = jnp.concatenate(
        [g32[blocks - 1], jnp.zeros((8, cols), F32)], axis=0
    ).astype(BF16)
    gp[1, rows:] = jnp.zeros((gp.shape[1] - rows, cols), BF16)
    v16 = v32[...].reshape(rows, cols).astype(BF16)
    v_flip = lax.dot_general(
        flip, v16, (((1,), (1,)), ((), ())), preferred_element_type=F32
    ).astype(BF16)
    upper = sub_r + sub_s >= LANES - 1

    def diagonal(tile):
        turned = pltpu.roll(tile, 1, 1, stride=1, stride_axis=0)
        return jnp.sum(turned, axis=0, keepdims=True) * scale

    def lags(depth, group, carry):
        last_mid, last_corner = carry
        prods = []
        for i in range(UNROLL // 2):
            for parity in (0, 1):
                offset = pl.multiple_of((group * (UNROLL // 2) + i) * 16, 16)
                right = gp[parity, pl.ds(offset, depth), :]
                prods.append(jnp.dot(v_flip[:, :depth], right, preferred_element_type=F32))
        for i in range(UNROLL // 2):
            for parity in (0, 1):
                prod = prods[2 * i + parity]
                edge = last_corner + prod[:LANES, :LANES]
                mid = prod[LANES:, :LANES] + prod[:LANES, LANES:]
                pair = group * (UNROLL // 2) + i
                fgs[parity, pair, :, :LANES] = diagonal(jnp.where(upper, last_mid, edge))
                fgs[parity, pair, :, LANES:] = diagonal(jnp.where(upper, edge, mid))
                last_mid, last_corner = mid, prod[LANES:, LANES:]
        return last_mid, last_corner

    carry = (jnp.zeros((LANES, LANES), F32),) * 2
    turns = blocks // UNROLL
    carry = lax.fori_loop(0, turns // 2, partial(lags, rows), carry)

    drain(tgot, half - 1, tsem.at[0, 1])
    for other in range(half):
        tall[other : other + 1, :] = tgot[other]
    every = tall[...]
    squares = jnp.sum(jnp.sum(every * every, axis=0, keepdims=True), axis=1, keepdims=True)

    @pl.when(me == lead)
    def _():
        tdp[mine] = jnp.broadcast_to(squares, (1, LANES))

        @pl.loop(1, replicas)
        def _(step):
            peer = lax.rem(mine + step, replicas)
            pltpu.make_async_remote_copy(
                src_ref=tdp.at[mine], dst_ref=tdp.at[mine],
                send_sem=dsem.at[0], recv_sem=dsem.at[1],
                device_id={"dp": peer}, device_id_type=MESH,
            ).start()

    send_some(ipack, igot, isem, PART, blocks)

    carry = lax.fori_loop(turns // 2, turns, partial(lags, rows // 2), carry)
    last_mid, last_corner = carry
    fgs[0, half, :, :LANES] = diagonal(jnp.where(upper, last_mid, last_corner))
    fgs[0, half, :, LANES:] = diagonal(jnp.where(upper, last_corner, 0.0))

    swap_f = to_seq(fgs.at[side, pl.ds(1 - side, half)], fx, fsem.at[0], sibling)
    swap_f.start()

    swap_f.wait()
    fsum[...] = fgs[1 - side, pl.ds(side, half)] + fx[...]
    keep_f = pltpu.make_async_copy(fsum.at[chip], fgot.at[chip], own.at[2])
    keep_f.start()

    @pl.loop(1, half)
    def _(step):
        there = lax.rem(chip + step, half)
        to_seq(fsum.at[there], fgot.at[chip], fsem.at[1], 2 * there + side).start()


    def share(peer):
        return to_seq(tnorm, tnorm, tsem.at[2], peer)

    @pl.when(me == lead)
    def _():
        drain(tdp, replicas - 1, dsem.at[0])
        drain(tdp, replicas - 1, dsem.at[1])
        total = tdp[0]
        for other in range(1, replicas):
            total = total + tdp[other]
        tnorm[...] = total

        @pl.loop(1, blocks)
        def _(step):
            share(lax.rem(me + step, blocks)).start()

    width = blocks * 8
    pick_k = lax.broadcasted_iota(jnp.int32, (LANES, width), 0)
    pick_l = lax.broadcasted_iota(jnp.int32, (LANES, width), 1)
    pick_l = lax.rem(pick_l, 8) + 48 * lax.rem(pick_l // 8, 2)
    own_i = lax.broadcasted_iota(jnp.int32, (half, width), 0)
    own_l = lax.broadcasted_iota(jnp.int32, (half, width), 1) // 16
    for j in range(6):
        pick = jnp.where(pick_k == 8 * j + pick_l, 1.0, 0.0)
        spread = jnp.dot(every, pick, precision=lax.Precision.HIGHEST, preferred_element_type=F32)
        line = jnp.sum(jnp.where(own_i == own_l, spread, 0.0), axis=0, keepdims=True)
        t_vmem[j : j + 1, :] = line

    @pl.when(me != lead)
    def _():
        share(lead).wait_recv()

    factor = lax.rsqrt(tnorm[:, :1] * norm + 1e-05)
    t_vmem[...] = t_vmem[...] * factor
    keep_t = pltpu.make_async_copy(t_vmem, t_out, own.at[3])
    keep_t.start()

    for keep in (keep_l, keep_i, keep_f, keep_t):
        keep.wait()
    drain(hpack, half - 1, hsem.at[0, 0])
    for ref, sems in ((xpack, xsem), (upack, usem), (lpack, lsem), (ipack, isem)):
        drain(ref, blocks - 1, sems.at[0])
    drain(tgot, half - 1, tsem.at[0, 0])

    @pl.when(me == lead)
    def _():
        @pl.loop(1, blocks)
        def _(step):
            share(lax.rem(me + step, blocks)).wait_send()

    drain(fsum, half - 1, fsem.at[1, 0])
    drain(lgot, blocks - 1, lsem.at[1])
    drain(fgot, half - 1, fsem.at[1, 1])
    drain(igot, blocks - 1, isem.at[1])


def deliver(lgot, igot, fgot, taps, lo_out, ig_out, vt_out, gt_out, f_out):
    blocks = lgot.shape[0]
    from_messages(lgot, lo_out, blocks)
    from_messages(igot, ig_out, blocks)
    for row in range(fgot.shape[0]):
        f_out[row : row + 1, :] = fgot[row]
    vt_out[...] = taps[:3]
    gt_out[...] = taps[3:]


def per_device(layer_in, cotangent, value_taps, gate_taps, long_filter):
    chans, cols = layer_in.shape
    blocks = lax.axis_size("seq")
    replicas = lax.axis_size("dp")
    half = blocks // 2
    scale = 1.0 / math.sqrt(GROUP * blocks * cols)
    norm = 1.0 / (6 * chans * replicas)
    vmem = pl.BlockSpec(memory_space=pltpu.VMEM)
    anywhere = pl.BlockSpec(memory_space=pl.ANY)
    dma = pltpu.SemaphoreType.DMA
    message = pltpu.VMEM((blocks, 16, LANES), BF16)
    wide = pltpu.VMEM((blocks, 8, cols), F32)
    lines = pltpu.VMEM((half, 1, cols), F32)
    raw = pl.pallas_call(
        partial(kernel, blocks, replicas, scale, norm),
        out_shape=(
            jax.ShapeDtypeStruct((blocks, 16, LANES), BF16),
            jax.ShapeDtypeStruct((blocks, 16, LANES), BF16),
            jax.ShapeDtypeStruct((half, 1, cols), F32),
            jax.ShapeDtypeStruct((6, chans), F32),
        ),
        in_specs=[anywhere] * 5,
        out_specs=(anywhere,) * 4,
        scratch_shapes=[
            pltpu.VMEM((chans, cols), BF16),
            pltpu.VMEM((chans, cols), BF16),
            pltpu.VMEM((half, cols), BF16),
            pltpu.VMEM((3, chans), F32),
            pltpu.VMEM((3, chans), F32),
            lines,
            pltpu.VMEM((2, half, 1, cols), F32),
            *([message] * 6),
            pltpu.VMEM((blocks, cols, cols), BF16),
            pltpu.VMEM((half + STACK // 2, 16, STACK * cols), BF16),
            pltpu.VMEM((blocks + STACK * (TURNS - 1), 8, cols), F32),
            *([wide] * 4),
            pltpu.VMEM((2, 2 * blocks * 8, cols), BF16),
            pltpu.VMEM((2, half + 1, 1, cols), F32),
            lines,
            lines,
            pltpu.VMEM((2, 1, LANES), F32),
            pltpu.VMEM((replicas, 1, LANES), F32),
            pltpu.VMEM((1, LANES), F32),
            pltpu.VMEM((half, 1, LANES), F32),
            pltpu.VMEM((half, LANES), F32),
            pltpu.VMEM((6, chans), F32),
            dma((5,)),
            dma((2, 2)),
            dma((2,)),
            dma((2,)),
            dma((2,)),
            dma((2,)),
            dma((2, 2)),
            dma((2,)),
            dma((3, 2)),
            dma((4,)),
        ],
        compiler_params=pltpu.CompilerParams(
            collective_id=0, has_side_effects=True, vmem_limit_bytes=VMEM_LIMIT
        ),
        name="hyena",
    )(layer_in, cotangent, long_filter, value_taps, gate_taps)
    return pl.pallas_call(
        deliver,
        out_shape=(
            jax.ShapeDtypeStruct((chans, cols), BF16),
            jax.ShapeDtypeStruct((chans, cols), BF16),
            jax.ShapeDtypeStruct((3, chans), F32),
            jax.ShapeDtypeStruct((3, chans), F32),
            jax.ShapeDtypeStruct((half, cols), F32),
        ),
        in_specs=[vmem] * 4,
        out_specs=(vmem,) * 5,
        compiler_params=pltpu.CompilerParams(vmem_limit_bytes=VMEM_LIMIT),
        name="deliver",
    )(*raw)


def solution(mesh):
    placed = (P("dp", "seq"), P("dp", "seq"), P(None, "dp"), P(None, "dp"), P("dp", "seq"))
    return jax.shard_map(
        per_device,
        mesh=mesh,
        in_specs=placed,
        out_specs=(P("dp", "seq"), P("dp", "seq"), P(None, "dp"), P(None, "dp"), P("dp", "seq")),
        check_vma=False,
    )
```

time: 88.2 us -> 81.4 us (0.923)
  local copies, waits for them, and re-layouts: 7.22 us -> 0 us
    unnamed x15 -> x0, local copies, waits for them, and re-layouts: 7.22 us -> none
    pallas_call x0 -> x1, Pallas kernels: none -> 2.19 us  [per_device(): pl.pallas_call(deliver, out_shape=(jax.ShapeDtypeStruct((chans, cols), BF...]
    pallas_call x1, Pallas kernels: 80 us -> 78.3 us  [per_device(): pl.pallas_call(partial(kernel, blocks, replicas, scale, norm), out_shape=...]
where the time goes in v3:
time: 81.4 us; the launch traced here: 81.2 us
  Pallas kernels  80.5 us (99%)
    pallas_call x1, Pallas kernels, per_device(): pl.pallas_call(partial(kernel, blocks, replicas, scale, norm), out_shape=...  78.3 us
    pallas_call x1, Pallas kernels, per_device(): pl.pallas_call(deliver, out_shape=(jax.ShapeDtypeStruct((chans, cols), BF...  2.19 us

profile of v3, /device:TPU:1, one launch (start us, length us, event | category | flops | bytes accessed | tf_op | source)
XLA Modules:
  0.0 81.2 jit_solution(6143522871650518301)
XLA Ops:
  0.6 78.3 %hyena.1 = (bf16[64,16,128]{2,1,0:T(8,128)(2,1)}, bf16[64,16,128]{2,1,0:T(8,128)(2,1)}, f32[32,1,256]{2,1,0:T(1,128)}, f32[6,512]{1,0:T(8,128)}) custom-call(bf16[512,256]{1,0:T(8,128)(2,1)} %x_hbm.1, bf16[512,256]{1,0:T(8,128)(2,1)} %u_hbm.1, bf16[32,256]{1,0:T(8,128)(2,1)} %h_hbm.1, f32[3,512]{1,0:T(4,128)} %vt_hbm.1, f32[3,512]{1,0:T(4,128)} %gt_hbm.1), custom_call_target="tpu_custom_call" | custom-call | tf_op jit(solution)/shard_map/hyena/pallas_call | solution.py:458
  79.0 2.2 %deliver.1 = (bf16[512,256]{1,0:T(8,128)(2,1)}, bf16[512,256]{1,0:T(8,128)(2,1)}, f32[3,512]{1,0:T(4,128)}, f32[3,512]{1,0:T(4,128)}, f32[32,256]{1,0:T(8,128)}) custom-call(bf16[64,16,128]{2,1,0:T(8,128)(2,1)} %get-tuple-element.9.lgot, bf16[64,16,128]{2,1,0:T(8,128)(2,1)} %get-tuple-element.10.igot, f32[32,1,256]{2,1,0:T(1,128)} %get-tuple-element.11.fgot, ...), custom_call_target="tpu_custom_call" | custom-call | tf_op jit(solution)/shard_map/deliver/pallas_call | solution.py:507

commit v4 on v3

--- a/solution.py
+++ b/solution.py
@@ -15,6 +15,7 @@
 UNROLL = 4
 TURNS = 2
 PART = 40
+PLANE = 8
 MESH = pl.DeviceIdType.MESH
 VMEM_LIMIT = 60 * 1024 * 1024
 F32 = jnp.float32
@@ -98,6 +99,7 @@
 ):
     cols = x_hbm.shape[1]
     half = blocks // 2
+    levels = blocks // PLANE
     rows = blocks * 8
     me = lax.axis_index("seq")
     mine = lax.axis_index("dp")
@@ -326,9 +328,10 @@
                 prod = prods[2 * i + parity]
                 edge = last_corner + prod[:LANES, :LANES]
                 mid = prod[LANES:, :LANES] + prod[:LANES, LANES:]
-                pair = group * (UNROLL // 2) + i
-                fgs[parity, pair, :, :LANES] = diagonal(jnp.where(upper, last_mid, edge))
-                fgs[parity, pair, :, LANES:] = diagonal(jnp.where(upper, edge, mid))
+                block = group * UNROLL + 2 * i - 1 + parity + PLANE
+                spot, level = lax.rem(block, PLANE), block // PLANE
+                fgs[spot, level, :, :LANES] = diagonal(jnp.where(upper, last_mid, edge))
+                fgs[spot, level, :, LANES:] = diagonal(jnp.where(upper, edge, mid))
                 last_mid, last_corner = mid, prod[LANES:, LANES:]
         return last_mid, last_corner
 
@@ -359,38 +362,16 @@
 
     carry = lax.fori_loop(turns // 2, turns, partial(lags, rows // 2), carry)
     last_mid, last_corner = carry
-    fgs[0, half, :, :LANES] = diagonal(jnp.where(upper, last_mid, last_corner))
-    fgs[0, half, :, LANES:] = diagonal(jnp.where(upper, last_corner, 0.0))
-
-    swap_f = to_seq(fgs.at[side, pl.ds(1 - side, half)], fx, fsem.at[0], sibling)
-    swap_f.start()
-
-    swap_f.wait()
-    fsum[...] = fgs[1 - side, pl.ds(side, half)] + fx[...]
-    keep_f = pltpu.make_async_copy(fsum.at[chip], fgot.at[chip], own.at[2])
-    keep_f.start()
-
-    @pl.loop(1, half)
+    fgs[PLANE - 1, levels, :, :LANES] = diagonal(jnp.where(upper, last_mid, last_corner))
+    fgs[PLANE - 1, levels, :, LANES:] = diagonal(jnp.where(upper, last_corner, 0.0))
+
+    seat, floor = lax.rem(me, PLANE), me // PLANE
+
+    @pl.loop(1, PLANE)
     def _(step):
-        there = lax.rem(chip + step, half)
-        to_seq(fsum.at[there], fgot.at[chip], fsem.at[1], 2 * there + side).start()
-
-
-    def share(peer):
-        return to_seq(tnorm, tnorm, tsem.at[2], peer)
-
-    @pl.when(me == lead)
-    def _():
-        drain(tdp, replicas - 1, dsem.at[0])
-        drain(tdp, replicas - 1, dsem.at[1])
-        total = tdp[0]
-        for other in range(1, replicas):
-            total = total + tdp[other]
-        tnorm[...] = total
-
-        @pl.loop(1, blocks)
-        def _(step):
-            share(lax.rem(me + step, blocks)).start()
+        there = lax.rem(seat + step, PLANE)
+        source = fgs.at[there, pl.ds(1, levels)]
+        to_seq(source, fx.at[seat], fsem.at[0], floor * PLANE + there).start()
 
     width = blocks * 8
     pick_k = lax.broadcasted_iota(jnp.int32, (LANES, width), 0)
@@ -404,9 +385,49 @@
         line = jnp.sum(jnp.where(own_i == own_l, spread, 0.0), axis=0, keepdims=True)
         t_vmem[j : j + 1, :] = line
 
+    fx[seat] = fgs[seat, pl.ds(1, levels)]
+    drain(fx, PLANE - 1, fsem.at[0, 1])
+    for x in range(PLANE // 2):
+        fsum[:, x] = fx[2 * x] + fx[2 * x + 1]
+    mine_f = pl.ds(floor * (PLANE // 2), PLANE // 2)
+    keep_f = pltpu.make_async_copy(fsum.at[floor], fgot.at[mine_f], own.at[2])
+    keep_f.start()
+
+    @pl.loop(1, levels)
+    def _(step):
+        there = lax.rem(floor + step, levels)
+        to_seq(fsum.at[there], fgot.at[mine_f], fsem.at[1], there * PLANE + seat).start()
+
+    def share(peer):
+        return to_seq(tnorm, tnorm, tsem.at[2], peer)
+
+    def each_floor(act):
+        @pl.loop(1, levels)
+        def _(step):
+            act(share(lax.rem(floor + step, levels) * PLANE + seat))
+
+    def each_seat(act):
+        @pl.loop(1, PLANE)
+        def _(step):
+            act(share(floor * PLANE + lax.rem(seat + step, PLANE)))
+
+    @pl.when(me == lead)
+    def _():
+        drain(tdp, replicas - 1, dsem.at[0])
+        drain(tdp, replicas - 1, dsem.at[1])
+        total = tdp[0]
+        for other in range(1, replicas):
+            total = total + tdp[other]
+        tnorm[...] = total
+        each_floor(lambda copy: copy.start())
+
     @pl.when(me != lead)
     def _():
         share(lead).wait_recv()
+
+    @pl.when(seat == lead % PLANE)
+    def _():
+        each_seat(lambda copy: copy.start())
 
     factor = lax.rsqrt(tnorm[:, :1] * norm + 1e-05)
     t_vmem[...] = t_vmem[...] * factor
@@ -422,13 +443,16 @@
 
     @pl.when(me == lead)
     def _():
-        @pl.loop(1, blocks)
-        def _(step):
-            share(lax.rem(me + step, blocks)).wait_send()
-
-    drain(fsum, half - 1, fsem.at[1, 0])
+        each_floor(lambda copy: copy.wait_send())
+
+    @pl.when(seat == lead % PLANE)
+    def _():
+        each_seat(lambda copy: copy.wait_send())
+
+    drain(fx, PLANE - 1, fsem.at[0, 0])
+    drain(fsum, levels - 1, fsem.at[1, 0])
     drain(lgot, blocks - 1, lsem.at[1])
-    drain(fgot, half - 1, fsem.at[1, 1])
+    drain(fgot, (levels - 1) * (PLANE // 2), fsem.at[1, 1])
     drain(igot, blocks - 1, isem.at[1])
 
 
@@ -479,9 +503,9 @@
             pltpu.VMEM((blocks + STACK * (TURNS - 1), 8, cols), F32),
             *([wide] * 4),
             pltpu.VMEM((2, 2 * blocks * 8, cols), BF16),
-            pltpu.VMEM((2, half + 1, 1, cols), F32),
-            lines,
-            lines,
+            pltpu.VMEM((PLANE, blocks // PLANE + 1, 1, cols), F32),
+            pltpu.VMEM((PLANE, blocks // PLANE, 1, cols), F32),
+            pltpu.VMEM((blocks // PLANE, PLANE // 2, 1, cols), F32),
             pltpu.VMEM((2, 1, LANES), F32),
             pltpu.VMEM((replicas, 1, LANES), F32),
             pltpu.VMEM((1, LANES), F32),

time: 81.4 us -> 82.3 us (1.011)
  Pallas kernels: 80.5 us -> 81.5 us
    pallas_call x1, Pallas kernels: 78.3 us -> 79.3 us  [per_device(): pl.pallas_call(partial(kernel, blocks, replicas, scale, norm), out_shape=...]
where the time goes in v4:
time: 82.3 us; the launch traced here: 82.1 us
  Pallas kernels  81.5 us (99%)
    pallas_call x1, Pallas kernels, per_device(): pl.pallas_call(partial(kernel, blocks, replicas, scale, norm), out_shape=...  79.3 us
    pallas_call x1, Pallas kernels, per_device(): pl.pallas_call(deliver, out_shape=(jax.ShapeDtypeStruct((chans, cols), BF...  2.19 us

profile of v4, /device:TPU:1, one launch (start us, length us, event | category | flops | bytes accessed | tf_op | source)
XLA Modules:
  0.0 82.1 jit_solution(15116703691639419469)
XLA Ops:
  0.6 79.3 %hyena.1 = (bf16[64,16,128]{2,1,0:T(8,128)(2,1)}, bf16[64,16,128]{2,1,0:T(8,128)(2,1)}, f32[32,1,256]{2,1,0:T(1,128)}, f32[6,512]{1,0:T(8,128)}) custom-call(bf16[512,256]{1,0:T(8,128)(2,1)} %x_hbm.1, bf16[512,256]{1,0:T(8,128)(2,1)} %u_hbm.1, bf16[32,256]{1,0:T(8,128)(2,1)} %h_hbm.1, f32[3,512]{1,0:T(4,128)} %vt_hbm.1, f32[3,512]{1,0:T(4,128)} %gt_hbm.1), custom_call_target="tpu_custom_call" | custom-call | tf_op jit(solution)/shard_map/hyena/pallas_call | solution.py:482
  79.9 2.2 %deliver.1 = (bf16[512,256]{1,0:T(8,128)(2,1)}, bf16[512,256]{1,0:T(8,128)(2,1)}, f32[3,512]{1,0:T(4,128)}, f32[3,512]{1,0:T(4,128)}, f32[32,256]{1,0:T(8,128)}) custom-call(bf16[64,16,128]{2,1,0:T(8,128)(2,1)} %get-tuple-element.9.lgot, bf16[64,16,128]{2,1,0:T(8,128)(2,1)} %get-tuple-element.10.igot, f32[32,1,256]{2,1,0:T(1,128)} %get-tuple-element.11.fgot, ...), custom_call_target="tpu_custom_call" | custom-call | tf_op jit(solution)/shard_map/deliver/pallas_call | solution.py:531

commit v5 on v3

--- a/solution.py
+++ b/solution.py
@@ -135,7 +135,8 @@
     def send_some(pack, got, sems, first, last):
         @pl.loop(first, last)
         def _(step):
-            peer = lax.rem(me + step, blocks)
+            away = (step + 1) // 2
+            peer = lax.rem(me + jnp.where(lax.rem(step, 2) == 1, away, blocks - away), blocks)
             to_seq(pack.at[peer], got.at[me], sems, peer).start()
 
     def drain(ref, count, sem):

time: 81.4 us -> 79 us (0.971)
  Pallas kernels: 80.5 us -> 78.1 us
    pallas_call x1, Pallas kernels: 78.3 us -> 76 us  [per_device(): pl.pallas_call(partial(kernel, blocks, replicas, scale, norm), out_shape=...]
where the time goes in v5:
time: 79 us; the launch traced here: 78.8 us
  Pallas kernels  78.1 us (99%)
    pallas_call x1, Pallas kernels, per_device(): pl.pallas_call(partial(kernel, blocks, replicas, scale, norm), out_shape=...  76 us
    pallas_call x1, Pallas kernels, per_device(): pl.pallas_call(deliver, out_shape=(jax.ShapeDtypeStruct((chans, cols), BF...  2.19 us

profile of v5, /device:TPU:1, one launch (start us, length us, event | category | flops | bytes accessed | tf_op | source)
XLA Modules:
  0.0 78.8 jit_solution(5742036564886696549)
XLA Ops:
  0.6 76.0 %hyena.1 = (bf16[64,16,128]{2,1,0:T(8,128)(2,1)}, bf16[64,16,128]{2,1,0:T(8,128)(2,1)}, f32[32,1,256]{2,1,0:T(1,128)}, f32[6,512]{1,0:T(8,128)}) custom-call(bf16[512,256]{1,0:T(8,128)(2,1)} %x_hbm.1, bf16[512,256]{1,0:T(8,128)(2,1)} %u_hbm.1, bf16[32,256]{1,0:T(8,128)(2,1)} %h_hbm.1, f32[3,512]{1,0:T(4,128)} %vt_hbm.1, f32[3,512]{1,0:T(4,128)} %gt_hbm.1), custom_call_target="tpu_custom_call" | custom-call | tf_op jit(solution)/shard_map/hyena/pallas_call | solution.py:459
  76.6 2.2 %deliver.1 = (bf16[512,256]{1,0:T(8,128)(2,1)}, bf16[512,256]{1,0:T(8,128)(2,1)}, f32[3,512]{1,0:T(4,128)}, f32[3,512]{1,0:T(4,128)}, f32[32,256]{1,0:T(8,128)}) custom-call(bf16[64,16,128]{2,1,0:T(8,128)(2,1)} %get-tuple-element.9.lgot, bf16[64,16,128]{2,1,0:T(8,128)(2,1)} %get-tuple-element.10.igot, f32[32,1,256]{2,1,0:T(1,128)} %get-tuple-element.11.fgot, ...), custom_call_target="tpu_custom_call" | custom-call | tf_op jit(solution)/shard_map/deliver/pallas_call | solution.py:508
